TPU v7x, 32 devices: a whole 2x2x4 slice. The times are simulated.
32 devices in a mesh: tile: 16 (over z, y, core), sun: 2 (over x).
Axes of the slice: x: 2, y: 2, z: 4, core: 2. Of those that a mesh axis runs over, the one named last changes fastest.
Arguments:
- heights: float32 [2048, 1024], P('tile', 'sun'), may hold values from 0 to 31.5, as said below
- classes: int32 [2048, 1024], P('tile', 'sun'), may hold values from 0 to 15
- rate_table: float32 [2, 16], replicated, may hold values from 0.03 to 0.24
- anomaly: float32 [2, 2048, 1024], P(None, 'tile', 'sun'), may hold values from -16 to 16
- view_coef: bfloat16 [3, 2048, 1024], P(None, 'tile', 'sun'), may hold values from 0.099609375 to 0.8984375
- sun_geometry: int32 [2, 4], P('sun'), may hold values from -1 to 24
- sun_radiation: float32 [2, 3], P('sun'), may hold values from 50 to 900, as said below
- record_tile: int32 [32768, 1], P(('tile', 'sun')), may hold values from 0 to 15; in each aligned block of 1024 rows (0 to 1023, 1024 to 2047, ...) at most 128 rows name the same one
- record_cell: int32 [32768], P(('tile', 'sun')), may hold values from 0 to 131071
- record_air: float32 [32768], P(('tile', 'sun')), may hold values from 20 to 35
Outputs:
- radiant_temp: float32 [2, 2048, 1024], P('sun', 'tile')
- record_excess: float32 [32768], P(('tile', 'sun'))
Inputs may be any that keep to these rules, and one draw needn't show every extreme that they name: `heights`: terrain on every cell; buildings and trees stand on scattered cells. `sun_radiation`: columns lie in 100 to 900, 50 to 250 and 300 to 420. `record_tile`: among the records of one device at most 128 name one tile, and in every draw some tile is named 128 times by one device.
All inputs are finite; a program needn't handle non-finite values.
Results may differ from a plain program's by a relative error of at most 0.0003.
Values sent between devices are 32-bit elements; how exact they have to be, the bound alone decides.
A program may use at most 64 MiB of HBM per device.

v0:
```python
import jax
import jax.numpy as jnp
from jax import lax
from jax.sharding import PartitionSpec as P

MAXSTEP = 24
HEAT_STEPS = 4


SIGMA = 5.67e-08
BASE_KELVIN = 300.0
ZERO_CELSIUS = 273.15


def with_halo(value, sides, width):
    for axis, dim in sides:
        peers, length = (lax.axis_size(axis), value.shape[dim])
        up = [(i, (i + 1) % peers) for i in range(peers - 1)]
        down = [(j, i) for i, j in up]
        last = lax.slice_in_dim(value, length - width, length, axis=dim)
        initial = lax.slice_in_dim(value, 0, width, axis=dim)
        before = lax.ppermute(last, axis, up)
        after = lax.ppermute(initial, axis, down)
        value = jnp.concatenate([before, value, after], axis=dim)
    return value


def diffusion_rates(classes, rate_table):
    levels = jnp.arange(rate_table.shape[1], dtype=jnp.int32)
    onehot = (classes[None, :, :] == levels[:, None, None]).astype(jnp.float32)
    return jnp.einsum("gc,cij->gij", rate_table, onehot, precision=lax.Precision.HIGHEST)


def heat_update(padded, rate_field):
    centre = padded[:, 1:-1, 1:-1]
    beside_all = (
        padded[:, :-2, 1:-1] + padded[:, 2:, 1:-1] + padded[:, 1:-1, :-2] + padded[:, 1:-1, 2:]
    )
    return centre + rate_field * (beside_all - 4.0 * centre)


def sunlit_share(extended, row_count, col_count, geometry):
    centre = extended[MAXSTEP : MAXSTEP + row_count, MAXSTEP : MAXSTEP + col_count]
    rise = 0.1 * geometry[2].astype(jnp.float32)

    def mark_step(offset, depth):
        start_row = MAXSTEP + geometry[0] * offset
        start_col = MAXSTEP + geometry[1] * offset
        caster = lax.dynamic_slice(extended, (start_row, start_col), (row_count, col_count))
        excess = caster - centre - rise * offset.astype(jnp.float32)
        excess = jnp.where(offset <= geometry[3], excess, jnp.float32(-100.0))
        return jnp.maximum(depth, excess)

    depth = lax.fori_loop(
        1, MAXSTEP + 1, mark_step, jnp.full((row_count, col_count), -100.0, jnp.float32)
    )
    return jnp.clip(0.5 - 0.5 * depth, 0.0, 1.0)


def radiant(sunlit, view_coef, surface, radiation):
    sky_view = view_coef[0]
    wall_view = view_coef[1]
    albedo = view_coef[2]
    direct = radiation[0]
    diffuse = radiation[1]
    sky_long = radiation[2]
    shortwave = 0.7 * (
        0.5 * direct * sunlit + diffuse * sky_view + (0.5 * direct + diffuse) * albedo * wall_view
    )
    ground_temp = BASE_KELVIN + surface[0]
    wall_temp = BASE_KELVIN + surface[1]
    ground_sq = ground_temp * ground_temp
    wall_sq = wall_temp * wall_temp
    longwave = 0.97 * (
        sky_view * sky_long
        + wall_view * SIGMA * wall_sq * wall_sq
        + (1.0 - sky_view) * SIGMA * ground_sq * ground_sq
    )
    absorbed = (shortwave + longwave) / (0.97 * SIGMA)
    return jnp.sqrt(jnp.sqrt(absorbed)) - ZERO_CELSIUS


def on_device(
    heights,
    classes,
    rate_table,
    anomaly,
    view_coef,
    sun_geometry,
    sun_radiation,
    record_tile,
    record_cell,
    record_air,
):
    row_count = heights.shape[0]
    rate_field = diffusion_rates(classes, rate_table)
    surface = anomaly
    for section in range(HEAT_STEPS):
        padded = with_halo(surface, (("tile", 1), ("sun", 2)), 1)
        surface = heat_update(padded, rate_field)
    heights_wide, view_wide = (
        lax.all_gather(heights, "sun", axis=1, tiled=True),
        lax.all_gather(view_coef.astype(jnp.float32), "sun", axis=2, tiled=True),
    )
    rows_ext = with_halo(heights_wide, (("tile", 0),), MAXSTEP)
    extended = jnp.pad(rows_ext, ((0, 0), (MAXSTEP, MAXSTEP)))
    surface_wide = lax.all_gather(surface, "sun", axis=2, tiled=True)
    sunlit = sunlit_share(extended, row_count, heights_wide.shape[1], sun_geometry[0])
    radiant_block = radiant(sunlit, view_wide, surface_wide, sun_radiation[0])[None]
    tile_count = lax.axis_size("tile")
    capacity = 2 * record_cell.shape[0] // tile_count
    target = record_tile[:, 0]
    levels = jnp.arange(tile_count, dtype=jnp.int32)
    onehot = (levels[:, None] == target[None, :]).astype(jnp.int32)
    ranking = jnp.sum(onehot * (jnp.cumsum(onehot, axis=1) - 1), axis=0)
    slot_index = target * capacity + ranking
    cell_buffer = jnp.zeros((tile_count * capacity,), jnp.int32).at[slot_index].set(record_cell)
    cell_buffer = cell_buffer.reshape(tile_count, capacity)
    flat_block = radiant_block.reshape(-1)
    values = jnp.take(
        flat_block,
        lax.all_to_all(cell_buffer, "tile", split_axis=0, concat_axis=0, tiled=True),
        axis=0,
    )
    returned = lax.all_to_all(values, "tile", split_axis=0, concat_axis=0, tiled=True)
    record_excess = returned.reshape(-1)[slot_index] - record_air
    return (radiant_block, record_excess)


def solution(mesh):
    return jax.shard_map(
        on_device,
        mesh=mesh,
        in_specs=(
            P("tile", "sun"),
            P("tile", "sun"),
            P(),
            P(None, "tile", "sun"),
            P(None, "tile", "sun"),
            P("sun", None),
            P("sun", None),
            P(("tile", "sun"), None),
            P(("tile", "sun")),
            P(("tile", "sun")),
        ),
        out_specs=(P("sun", "tile", None), P(("tile", "sun"))),
        check_vma=False,
    )
```

profile of v0, /device:TPU:0, one launch (start us, length us, event | category | flops | bytes accessed | tf_op | source)
XLA Modules:
  0.0 242.8 jit_solution(9315365762029656951)
XLA Ops:
  8.7 2.4 collective-permute-start.2
  13.9 2.4 collective-permute-done.3
  16.5 3.4 %collective-permute-start.4 = (f32[2,130,1]{2,0,1:T(2,128)S(1)}, f32[2,130,1]{2,0,1:T(2,128)S(1)}, u32[]{:S(2)}, u32[]{:S(2)}) collective-permute-start(f32[2,130,1]{2,0,1:T(2,128)S(1)} %get-tuple-element.202), channel_id=1, source_target_pairs={{0,1},{2,3},{4,5},{6,7},{8,9},{10,11},{12,13},{14,15},{16,17},{18,... | collective-permute-start | bytes 3128 | tf_op jit(solution)/shard_map/ppermute | solution.py:22
  22.4 4.7 %collective-permute-done.5 = f32[2,130,1]{2,0,1:T(2,128)S(1)} collective-permute-done((f32[2,130,1]{2,0,1:T(2,128)S(1)}, f32[2,130,1]{2,0,1:T(2,128)S(1)}, u32[]{:S(2)}, u32[]{:S(2)}) %collective-permute-start.5) | collective-permute-done | bytes 1072 | tf_op jit(solution)/shard_map/ppermute | solution.py:23
  27.1 3.8 %fusion.34 = (f32[2,128,512]{2,0,1:T(2,128)S(1)}, f32[2,128,512]{2,0,1:T(2,128)S(1)}) fusion(f32[2,128,512]{2,0,1:T(2,128)S(1)} %copy.29, f32[2,130,1]{2,0,1:T(2,128)S(1)} %collective-permute-done.5, f32[2,130,512]{2,0,1:T(2,128)S(1)} %constant_dynamic-update-slice_fusion, f32[2,130,1]{2,0,1:T(2,128)S(1)} %collective-permute-done.4, ...), kind=kOutput, calls=%fused_computation.71 | convolution fusion | flops 27656192 | bytes 2377888 | tf_op jit(solution)/shard_map/gc,cij->gij/dot_general | solution.py:31
  30.9 2.9 %collective-permute-start.6 = (f32[2,1,512]{2,0,1:T(2,128)S(1)}, f32[2,1,512]{2,0,1:T(2,128)S(1)}, u32[]{:S(2)}, u32[]{:S(2)}) collective-permute-start(f32[2,1,512]{2,0,1:T(2,128)S(1)} %get-tuple-element.210), channel_id=1, source_target_pairs={{0,2},{2,4},{4,6},{6,8},{8,10},{10,12},{12,14},{14,16},{16,18},{18... | collective-permute-start | bytes 12296 | tf_op jit(solution)/shard_map/ppermute | solution.py:22
  35.1 3.0 %collective-permute-done.7 = f32[2,1,512]{2,0,1:T(2,128)S(1)} collective-permute-done((f32[2,1,512]{2,0,1:T(2,128)S(1)}, f32[2,1,512]{2,0,1:T(2,128)S(1)}, u32[]{:S(2)}, u32[]{:S(2)}) %collective-permute-start.7) | collective-permute-done | bytes 4128 | tf_op jit(solution)/shard_map/ppermute | solution.py:23
  42.3 4.5 %collective-permute-done.9 = f32[2,130,1]{2,0,1:T(2,128)S(1)} collective-permute-done((f32[2,130,1]{2,0,1:T(2,128)S(1)}, f32[2,130,1]{2,0,1:T(2,128)S(1)}, u32[]{:S(2)}, u32[]{:S(2)}) %collective-permute-start.9) | collective-permute-done | bytes 1072 | tf_op jit(solution)/shard_map/ppermute | solution.py:23
  46.8 3.8 %fusion.28 = f32[2,128,512]{2,0,1:T(2,128)S(1)} fusion(f32[2,128,512]{2,0,1:T(2,128)S(1)} %get-tuple-element.217, f32[2,128,512]{2,0,1:T(2,128)S(1)} %get-tuple-element.218, f32[2,130,1]{2,0,1:T(2,128)S(1)} %collective-permute-done.9, f32[2,1,512]{2,0,1:T(2,128)S(1)} %collective-permute-done.7, f32[2,1,512]{2,0,1:T(2,128)S(1)} %collective-permute-done.6, ...), kind=kLoop, calls=%fused_computation.57 | loop fusion | flops 1966080 | bytes 1583136 | tf_op jit(solution)/shard_map/add | solution.py:39
  50.7 3.0 %collective-permute-start.10 = (f32[2,1,512]{2,0,1:T(2,128)S(1)}, f32[2,1,512]{2,0,1:T(2,128)S(1)}, u32[]{:S(2)}, u32[]{:S(2)}) collective-permute-start(f32[2,1,512]{2,0,1:T(2,128)S(1)} %get-tuple-element.208), channel_id=1, source_target_pairs={{0,2},{2,4},{4,6},{6,8},{8,10},{10,12},{12,14},{14,16},{16,18},{18... | collective-permute-start | bytes 12296 | tf_op jit(solution)/shard_map/ppermute | solution.py:22
  55.0 2.8 %collective-permute-done.11 = f32[2,1,512]{2,0,1:T(2,128)S(1)} collective-permute-done((f32[2,1,512]{2,0,1:T(2,128)S(1)}, f32[2,1,512]{2,0,1:T(2,128)S(1)}, u32[]{:S(2)}, u32[]{:S(2)}) %collective-permute-start.11) | collective-permute-done | bytes 4128 | tf_op jit(solution)/shard_map/ppermute | solution.py:23
  58.0 1.5 collective-permute-start.12
  62.0 4.4 %collective-permute-done.13 = f32[2,130,1]{2,0,1:T(2,128)S(1)} collective-permute-done((f32[2,130,1]{2,0,1:T(2,128)S(1)}, f32[2,130,1]{2,0,1:T(2,128)S(1)}, u32[]{:S(2)}, u32[]{:S(2)}) %collective-permute-start.13) | collective-permute-done | bytes 1072 | tf_op jit(solution)/shard_map/ppermute | solution.py:23
  66.4 3.8 %fusion.22 = f32[2,128,512]{2,0,1:T(2,128)S(1)} fusion(f32[2,128,512]{2,0,1:T(2,128)S(1)} %fusion.28, f32[2,128,512]{2,0,1:T(2,128)S(1)} %get-tuple-element.218, f32[2,130,1]{2,0,1:T(2,128)S(1)} %collective-permute-done.13, f32[2,1,512]{2,0,1:T(2,128)S(1)} %collective-permute-done.11, f32[2,1,512]{2,0,1:T(2,128)S(1)} %collective-permute-done.10, ...), kind=kLoop, calls=%fused_computation.43 | loop fusion | flops 1966080 | bytes 1583136 | tf_op jit(solution)/shard_map/add | solution.py:39
  70.2 3.4 %collective-permute-start.14 = (f32[2,1,512]{2,0,1:T(2,128)S(1)}, f32[2,1,512]{2,0,1:T(2,128)S(1)}, u32[]{:S(2)}, u32[]{:S(2)}) collective-permute-start(f32[2,1,512]{2,0,1:T(2,128)S(1)} %get-tuple-element.206), channel_id=1, source_target_pairs={{0,2},{2,4},{4,6},{6,8},{8,10},{10,12},{12,14},{14,16},{16,18},{18... | collective-permute-start | bytes 12296 | tf_op jit(solution)/shard_map/ppermute | solution.py:22
  75.0 3.1 %collective-permute-done.15 = f32[2,1,512]{2,0,1:T(2,128)S(1)} collective-permute-done((f32[2,1,512]{2,0,1:T(2,128)S(1)}, f32[2,1,512]{2,0,1:T(2,128)S(1)}, u32[]{:S(2)}, u32[]{:S(2)}) %collective-permute-start.15) | collective-permute-done | bytes 4128 | tf_op jit(solution)/shard_map/ppermute | solution.py:23
  78.3 1.5 collective-permute-start.16
  82.3 4.4 %collective-permute-done.17 = f32[2,130,1]{2,0,1:T(2,128)S(1)} collective-permute-done((f32[2,130,1]{2,0,1:T(2,128)S(1)}, f32[2,130,1]{2,0,1:T(2,128)S(1)}, u32[]{:S(2)}, u32[]{:S(2)}) %collective-permute-start.17) | collective-permute-done | bytes 1072 | tf_op jit(solution)/shard_map/ppermute | solution.py:23
  86.7 4.5 %fusion.16 = f32[2,128,512]{2,0,1:T(2,128)} fusion(f32[2,128,512]{2,0,1:T(2,128)S(1)} %fusion.22, f32[2,128,512]{2,0,1:T(2,128)S(1)} %get-tuple-element.218, f32[2,130,1]{2,0,1:T(2,128)S(1)} %collective-permute-done.17, f32[2,1,512]{2,0,1:T(2,128)S(1)} %collective-permute-done.15, f32[2,1,512]{2,0,1:T(2,128)S(1)} %collective-permute-done.14, ...), kind=kLoop, calls=%fused_computation.29 | loop fusion | flops 1966080 | bytes 1583136 | tf_op jit(solution)/shard_map/add | solution.py:39
  91.2 9.6 %all_gather.9 = f32[128,1024]{1,0:T(8,128)S(1)} all-gather(f32[128,512]{1,0:T(8,128)S(1)} %copy-done.3), channel_id=1, replica_groups=mesh['tile'=16,'sun'=2] {'sun'}, dimensions={1}, use_global_device_ids=true | all-gather | bytes 786432 | tf_op jit(solution)/shard_map/all_gather | solution.py:102
  100.8 2.2 collective-permute-start
  104.6 4.5 %reduce-window.6 = s32[16,8,128]{2,1,0:T(8,128)S(1)} reduce-window(s32[16,8,128]{2,1,0:T(8,128)S(1)} %fusion.43, s32[]{:T(128)} %constant.108.clone.1), window={size=1x1x128 pad=0_0x0_0x127_0}, to_apply=%region_2.3 | reduce-window | flops 2080768 | bytes 131076 | tf_op jit(solution)/shard_map/reduce-window
  109.6 5.0 %scatter_custom_fusion = s32[2048]{0:T(1024)} fusion(s32[1024]{0:T(1024)S(1)} %bitcast.71, s32[1024]{0:T(1024)} %param.20, s32[]{:T(128)} %constant.108.clone.1), kind=kCustom, calls=%fused_computation.107 | custom fusion | bytes 8704 | tf_op jit(solution)/shard_map/scatter | solution.py:117
  114.6 9.0 %all-to-all-start = ((s32[16,1,128]{2,1,0:T(1,128)}), s32[16,1,128]{2,1,0:T(1,128)S(1)}, u32[]{:S(2)}, u32[]{:S(2)}) async-start(s32[16,1,128]{2,1,0:T(1,128)} %bitcast.18), calls=%async_computation | async-start | bytes 16384 | tf_op jit(solution)/shard_map/all_to_all | solution.py:122
  127.7 2.2 all-to-all-done
  130.3 70.2 %while.16 = (s32[]{:T(128)}, f32[128,1024]{1,0:T(8,128)S(1)}, s32[4]{0:T(128)S(1)}, f32[176,1072]{1,0:T(8,128)S(1)}, f32[128,1024]{1,0:T(8,128)S(1)}, /*index=5*...) while((s32[]{:T(128)}, f32[128,1024]{1,0:T(8,128)S(1)}, ...), condition=%wide.region_1.2_spmd.clone, body=%wide.region_0.1_spmd.clone.sunk | while | flops 655376 | bytes 2097461 | solution.py:54
  200.5 2.6 %fusion.12 = (f32[1,128,1024]{2,0,1:T(1,128)S(1)}, f32[1,128,1024]{2,0,1:T(1,128)S(1)}) fusion(f32[2,128,1024]{2,0,1:T(2,128)} %all-gather.5.cloned.1.call-done), kind=kLoop, calls=%fused_computation.24 | loop fusion | flops 262144 | bytes 2097152 | tf_op jit(solution)/shard_map/mul | solution.py:72
  203.1 3.3 %fusion.11 = f32[128,1024]{1,0:T(8,128)S(1)} fusion(f32[3,128,1024]{2,1,0:T(8,128)} %all-gather.3.cloned.1.call-done, f32[1,128,1024]{2,0,1:T(1,128)S(1)} %get-tuple-element.195, f32[1,128,1024]{2,0,1:T(1,128)S(1)} %get-tuple-element.194, f32[128,1024]{1,0:T(8,128)S(1)} %get-tuple-element.157, f32[]{:T(128)} %bitcast.6, f32[]{:T(128)S(6)} %add.183, ...), kind=kLoop, calls=%fused_computation.22 | loop fusion | flops 3407872 | bytes 3670032 | tf_op jit(solution)/shard_map/sub | solution.py:80
  206.5 11.8 %gather_fusion = f32[2048]{0:T(1024)S(1)} fusion(f32[131072]{0:T(1024)S(1)} %bitcast.61, s32[2048]{0:T(1024)S(1)} %fusion.45), kind=kCustom, calls=%fused_computation | custom fusion | bytes 24576 | tf_op jit(solution)/shard_map/jit(_take)/gather | solution.py:120
  219.0 3.8 %all-to-all-start.1 = ((f32[16,1,128]{2,1,0:T(1,128)}), f32[16,1,128]{2,1,0:T(1,128)S(1)}, u32[]{:S(2)}, u32[]{:S(2)}) async-start(f32[16,1,128]{2,1,0:T(1,128)} %and_select_fusion), calls=%async_computation.1 | async-start | bytes 16384 | tf_op jit(solution)/shard_map/all_to_all | solution.py:125
  222.8 6.4 %all-to-all-done.1 = f32[16,1,128]{2,1,0:T(1,128)S(1)} async-done(((f32[16,1,128]{2,1,0:T(1,128)}), f32[16,1,128]{2,1,0:T(1,128)S(1)}, u32[]{:S(2)}, u32[]{:S(2)}) %all-to-all-start.1) | async-done | bytes 8224 | tf_op jit(solution)/shard_map/all_to_all | solution.py:125
  229.2 6.1 %gather_fusion.1 = f32[1024]{0:T(1024)S(1)} fusion(f32[2048]{0:T(1024)S(1)} %bitcast.60, s32[1024]{0:T(1024)S(1)} %broadcast_clamp_fusion), kind=kCustom, calls=%fused_computation.1 | custom fusion | bytes 12288 | tf_op jit(solution)/shard_map/gather | solution.py:126
  (123 shorter events, 51.7 us)
Async XLA Ops:
  7.2 19.9 %copy-start = (f32[2,16]{1,0:T(2,128)S(1)}, f32[2,16]{1,0:T(2,128)}, u32[]{:S(2)}) copy-start(f32[2,16]{1,0:T(2,128)} %param.14) | copy-start | bytes 388
  7.2 19.9 %copy-start.8 = (s32[128,512]{1,0:T(8,128)S(1)}, s32[128,512]{1,0:T(8,128)}, u32[]{:S(2)}) copy-start(s32[128,512]{1,0:T(8,128)} %param.13) | copy-start | bytes 786436
  7.2 193.3 %all-gather.5.cloned.1.call-start = ((), (), s32[]{:S(2)}) async-start(), calls=%async_computation.3 | async-start | bytes 1572864 | tf_op jit(solution)/shard_map/all_gather | solution.py:107
  8.7 3.7 %collective-permute-start.2 = (f32[2,1,512]{2,0,1:T(2,128)S(1)}, f32[2,1,512]{2,0,1:T(2,128)S(1)}, u32[]{:S(2)}, u32[]{:S(2)}) collective-permute-start(f32[2,1,512]{2,0,1:T(2,128)S(1)} %get-tuple-element.213), channel_id=1, source_target_pairs={{0,2},{2,4},{4,6},{6,8},{8,10},{10,12},{12,14},{14,16},{16,18},{18... | collective-permute-start | bytes 12296 | tf_op jit(solution)/shard_map/ppermute | solution.py:22
  11.1 5.2 %collective-permute-start.3 = (f32[2,1,512]{2,0,1:T(2,128)S(1)}, f32[2,1,512]{2,0,1:T(2,128)S(1)}, u32[]{:S(2)}, u32[]{:S(2)}) collective-permute-start(f32[2,1,512]{2,0,1:T(2,128)S(1)} %get-tuple-element.212), channel_id=1, source_target_pairs={{2,0},{4,2},{6,4},{8,6},{10,8},{12,10},{14,12},{16,14},{18,16},{20... | collective-permute-start | bytes 12296 | tf_op jit(solution)/shard_map/ppermute | solution.py:23
  16.5 5.9 %collective-permute-start.4 = (f32[2,130,1]{2,0,1:T(2,128)S(1)}, f32[2,130,1]{2,0,1:T(2,128)S(1)}, u32[]{:S(2)}, u32[]{:S(2)}) collective-permute-start(f32[2,130,1]{2,0,1:T(2,128)S(1)} %get-tuple-element.202), channel_id=1, source_target_pairs={{0,1},{2,3},{4,5},{6,7},{8,9},{10,11},{12,13},{14,15},{16,17},{18,... | collective-permute-start | bytes 3128 | tf_op jit(solution)/shard_map/ppermute | solution.py:22
  19.9 7.2 %collective-permute-start.5 = (f32[2,130,1]{2,0,1:T(2,128)S(1)}, f32[2,130,1]{2,0,1:T(2,128)S(1)}, u32[]{:S(2)}, u32[]{:S(2)}) collective-permute-start(f32[2,130,1]{2,0,1:T(2,128)S(1)} %get-tuple-element.203), channel_id=1, source_target_pairs={{1,0},{3,2},{5,4},{7,6},{9,8},{11,10},{13,12},{15,14},{17,16},{19,... | collective-permute-start | bytes 3128 | tf_op jit(solution)/shard_map/ppermute | solution.py:23
  30.9 4.2 %collective-permute-start.6 = (f32[2,1,512]{2,0,1:T(2,128)S(1)}, f32[2,1,512]{2,0,1:T(2,128)S(1)}, u32[]{:S(2)}, u32[]{:S(2)}) collective-permute-start(f32[2,1,512]{2,0,1:T(2,128)S(1)} %get-tuple-element.210), channel_id=1, source_target_pairs={{0,2},{2,4},{4,6},{6,8},{8,10},{10,12},{12,14},{14,16},{16,18},{18... | collective-permute-start | bytes 12296 | tf_op jit(solution)/shard_map/ppermute | solution.py:22
  33.8 4.3 %collective-permute-start.7 = (f32[2,1,512]{2,0,1:T(2,128)S(1)}, f32[2,1,512]{2,0,1:T(2,128)S(1)}, u32[]{:S(2)}, u32[]{:S(2)}) collective-permute-start(f32[2,1,512]{2,0,1:T(2,128)S(1)} %get-tuple-element.211), channel_id=1, source_target_pairs={{2,0},{4,2},{6,4},{8,6},{10,8},{12,10},{14,12},{16,14},{18,16},{20... | collective-permute-start | bytes 12296 | tf_op jit(solution)/shard_map/ppermute | solution.py:23
  38.3 4.0 %collective-permute-start.8 = (f32[2,130,1]{2,0,1:T(2,128)S(1)}, f32[2,130,1]{2,0,1:T(2,128)S(1)}, u32[]{:S(2)}, u32[]{:S(2)}) collective-permute-start(f32[2,130,1]{2,0,1:T(2,128)S(1)} %get-tuple-element.200), channel_id=1, source_target_pairs={{0,1},{2,3},{4,5},{6,7},{8,9},{10,11},{12,13},{14,15},{16,17},{18,... | collective-permute-start | bytes 3128 | tf_op jit(solution)/shard_map/ppermute | solution.py:22
  39.8 7.0 %collective-permute-start.9 = (f32[2,130,1]{2,0,1:T(2,128)S(1)}, f32[2,130,1]{2,0,1:T(2,128)S(1)}, u32[]{:S(2)}, u32[]{:S(2)}) collective-permute-start(f32[2,130,1]{2,0,1:T(2,128)S(1)} %get-tuple-element.201), channel_id=1, source_target_pairs={{1,0},{3,2},{5,4},{7,6},{9,8},{11,10},{13,12},{15,14},{17,16},{19,... | collective-permute-start | bytes 3128 | tf_op jit(solution)/shard_map/ppermute | solution.py:23
  50.7 4.3 %collective-permute-start.10 = (f32[2,1,512]{2,0,1:T(2,128)S(1)}, f32[2,1,512]{2,0,1:T(2,128)S(1)}, u32[]{:S(2)}, u32[]{:S(2)}) collective-permute-start(f32[2,1,512]{2,0,1:T(2,128)S(1)} %get-tuple-element.208), channel_id=1, source_target_pairs={{0,2},{2,4},{4,6},{6,8},{8,10},{10,12},{12,14},{14,16},{16,18},{18... | collective-permute-start | bytes 12296 | tf_op jit(solution)/shard_map/ppermute | solution.py:22
  53.7 4.1 %collective-permute-start.11 = (f32[2,1,512]{2,0,1:T(2,128)S(1)}, f32[2,1,512]{2,0,1:T(2,128)S(1)}, u32[]{:S(2)}, u32[]{:S(2)}) collective-permute-start(f32[2,1,512]{2,0,1:T(2,128)S(1)} %get-tuple-element.209), channel_id=1, source_target_pairs={{2,0},{4,2},{6,4},{8,6},{10,8},{12,10},{14,12},{16,14},{18,16},{20... | collective-permute-start | bytes 12296 | tf_op jit(solution)/shard_map/ppermute | solution.py:23
  58.0 4.0 %collective-permute-start.12 = (f32[2,130,1]{2,0,1:T(2,128)S(1)}, f32[2,130,1]{2,0,1:T(2,128)S(1)}, u32[]{:S(2)}, u32[]{:S(2)}) collective-permute-start(f32[2,130,1]{2,0,1:T(2,128)S(1)} %get-tuple-element.198), channel_id=1, source_target_pairs={{0,1},{2,3},{4,5},{6,7},{8,9},{10,11},{12,13},{14,15},{16,17},{18,... | collective-permute-start | bytes 3128 | tf_op jit(solution)/shard_map/ppermute | solution.py:22
  59.5 6.9 %collective-permute-start.13 = (f32[2,130,1]{2,0,1:T(2,128)S(1)}, f32[2,130,1]{2,0,1:T(2,128)S(1)}, u32[]{:S(2)}, u32[]{:S(2)}) collective-permute-start(f32[2,130,1]{2,0,1:T(2,128)S(1)} %get-tuple-element.199), channel_id=1, source_target_pairs={{1,0},{3,2},{5,4},{7,6},{9,8},{11,10},{13,12},{15,14},{17,16},{19,... | collective-permute-start | bytes 3128 | tf_op jit(solution)/shard_map/ppermute | solution.py:23
  70.2 4.8 %collective-permute-start.14 = (f32[2,1,512]{2,0,1:T(2,128)S(1)}, f32[2,1,512]{2,0,1:T(2,128)S(1)}, u32[]{:S(2)}, u32[]{:S(2)}) collective-permute-start(f32[2,1,512]{2,0,1:T(2,128)S(1)} %get-tuple-element.206), channel_id=1, source_target_pairs={{0,2},{2,4},{4,6},{6,8},{8,10},{10,12},{12,14},{14,16},{16,18},{18... | collective-permute-start | bytes 12296 | tf_op jit(solution)/shard_map/ppermute | solution.py:22
  73.5 17.6 %copy-start.3 = (f32[128,512]{1,0:T(8,128)S(1)}, f32[128,512]{1,0:T(8,128)}, u32[]{:S(2)}) copy-start(f32[128,512]{1,0:T(8,128)} %param.12) | copy-start | bytes 786436
  73.6 4.6 %collective-permute-start.15 = (f32[2,1,512]{2,0,1:T(2,128)S(1)}, f32[2,1,512]{2,0,1:T(2,128)S(1)}, u32[]{:S(2)}, u32[]{:S(2)}) collective-permute-start(f32[2,1,512]{2,0,1:T(2,128)S(1)} %get-tuple-element.207), channel_id=1, source_target_pairs={{2,0},{4,2},{6,4},{8,6},{10,8},{12,10},{14,12},{16,14},{18,16},{20... | collective-permute-start | bytes 12296 | tf_op jit(solution)/shard_map/ppermute | solution.py:23
  78.3 4.0 %collective-permute-start.16 = (f32[2,130,1]{2,0,1:T(2,128)S(1)}, f32[2,130,1]{2,0,1:T(2,128)S(1)}, u32[]{:S(2)}, u32[]{:S(2)}) collective-permute-start(f32[2,130,1]{2,0,1:T(2,128)S(1)} %get-tuple-element.196), channel_id=1, source_target_pairs={{0,1},{2,3},{4,5},{6,7},{8,9},{10,11},{12,13},{14,15},{16,17},{18,... | collective-permute-start | bytes 3128 | tf_op jit(solution)/shard_map/ppermute | solution.py:22
  79.8 24.8 %copy-start.5 = (s32[1024,1]{0,1:T(1,128)S(1)}, s32[1024,1]{0,1:T(1,128)}, u32[]{:S(2)}) copy-start(s32[1024,1]{0,1:T(1,128)} %param.19) | copy-start | bytes 12292
  79.8 6.9 %collective-permute-start.17 = (f32[2,130,1]{2,0,1:T(2,128)S(1)}, f32[2,130,1]{2,0,1:T(2,128)S(1)}, u32[]{:S(2)}, u32[]{:S(2)}) collective-permute-start(f32[2,130,1]{2,0,1:T(2,128)S(1)} %get-tuple-element.197), channel_id=1, source_target_pairs={{1,0},{3,2},{5,4},{7,6},{9,8},{11,10},{13,12},{15,14},{17,16},{19,... | collective-permute-start | bytes 3128 | tf_op jit(solution)/shard_map/ppermute | solution.py:23
  91.2 32.4 %copy-start.2 = (bf16[3,128,512]{2,1,0:T(8,128)(2,1)S(1)}, bf16[3,128,512]{2,1,0:T(8,128)(2,1)}, u32[]{:S(2)}) copy-start(bf16[3,128,512]{2,1,0:T(8,128)(2,1)} %param.16) | copy-start | bytes 1179652
  100.8 23.8 %copy-start.6 = (f32[1,3]{1,0:T(1,128)S(1)}, f32[1,3]{1,0:T(1,128)}, u32[]{:S(2)}) copy-start(f32[1,3]{1,0:T(1,128)} %param.18) | copy-start | bytes 40
  100.8 24.5 %copy-start.4 = (s32[1,4]{1,0:T(1,128)S(1)}, s32[1,4]{1,0:T(1,128)}, u32[]{:S(2)}) copy-start(s32[1,4]{1,0:T(1,128)} %param.17) | copy-start | bytes 52
  100.8 29.1 %collective-permute-start = (f32[24,1024]{1,0:T(8,128)S(1)}, f32[24,1024]{1,0:T(8,128)S(1)}, u32[]{:S(2)}, u32[]{:S(2)}) collective-permute-start(f32[24,1024]{1,0:T(8,128)S(1)} %get-tuple-element.204), channel_id=1, source_target_pairs={{0,2},{2,4},{4,6},{6,8},{8,10},{10,12},{12,14},{14,16},{16,18},{18... | collective-permute-start | bytes 294920 | tf_op jit(solution)/shard_map/ppermute | solution.py:22
  103.1 26.9 %collective-permute-start.1 = (f32[24,1024]{1,0:T(8,128)S(1)}, f32[24,1024]{1,0:T(8,128)S(1)}, u32[]{:S(2)}, u32[]{:S(2)}) collective-permute-start(f32[24,1024]{1,0:T(8,128)S(1)} %get-tuple-element.205), channel_id=1, source_target_pairs={{2,0},{4,2},{6,4},{8,6},{10,8},{12,10},{14,12},{16,14},{18,16},{20... | collective-permute-start | bytes 294920 | tf_op jit(solution)/shard_map/ppermute | solution.py:23
  114.6 15.4 %all-to-all-start = ((s32[16,1,128]{2,1,0:T(1,128)}), s32[16,1,128]{2,1,0:T(1,128)S(1)}, u32[]{:S(2)}, u32[]{:S(2)}) async-start(s32[16,1,128]{2,1,0:T(1,128)} %bitcast.18), calls=%async_computation | async-start | bytes 16384 | tf_op jit(solution)/shard_map/all_to_all | solution.py:122
  123.6 79.5 %all-gather.3.cloned.1.call-start = ((), (), s32[]{:S(2)}) async-start(), calls=%async_computation.2 | async-start | bytes 2359296 | tf_op jit(solution)/shard_map/all_gather | solution.py:103
  206.4 11.9 %copy-start.1 = (f32[128,1024]{1,0:T(8,128)}, f32[128,1024]{1,0:T(8,128)S(1)}, u32[]{:S(2)}) copy-start(f32[128,1024]{1,0:T(8,128)S(1)} %fusion.11) | copy-start | bytes 1572868
  219.0 10.2 %all-to-all-start.1 = ((f32[16,1,128]{2,1,0:T(1,128)}), f32[16,1,128]{2,1,0:T(1,128)S(1)}, u32[]{:S(2)}, u32[]{:S(2)}) async-start(f32[16,1,128]{2,1,0:T(1,128)} %and_select_fusion), calls=%async_computation.1 | async-start | bytes 16384 | tf_op jit(solution)/shard_map/all_to_all | solution.py:125
  229.2 6.2 %copy-start.7 = (f32[1024]{0:T(1024)S(1)}, f32[1024]{0:T(1024)}, u32[]{:S(2)}) copy-start(f32[1024]{0:T(1024)} %param.21) | copy-start | bytes 12292
Sparse Core Ops, SparseCore 0:
  91.3 23.9 all-gather.4
  125.9 27.5 all-gather.2
where the time goes:
time: 244 us; the launch traced here: 243 us
  starting transfers between devices  46.4 us (19%)
  loops' own time  45.1 us (18%)
  waiting for transfers between devices  42.8 us (18%)
  local copies, waits for them, and re-layouts  42.7 us (18%)
  other arithmetic  36 us (15%)
  between operations  16.3 us (7%)
  blocking collectives  9.62 us (4%)
  matrix products  3.81 us (2%)
    another operation x1, loops' own time, sunlit_share(): lax.fori_loop(1, MAXSTEP + 1, mark_step, jnp.full((row_count, col_count),...  45.1 us
    ppermute x9, waiting for transfers between devices, with_halo(): after = lax.ppermute(initial, axis, down)  29.3 us
    ppermute x9, starting transfers between devices, with_halo(): before = lax.ppermute(last, axis, up)  21.6 us
    slice x24, local copies, waits for them, and re-layouts, mark_step(): excess = jnp.where(offset <= geometry[3], excess, jnp.float32(-100.0))  14.8 us
    add x3, other arithmetic, heat_update(): return centre + rate_field * (beside_all - 4.0 * centre)  12.1 us
    ppermute x9, starting transfers between devices, with_halo(): after = lax.ppermute(initial, axis, down)  11.9 us
    gather x1, local copies, waits for them, and re-layouts, on_device(): jnp.take(flat_block, lax.all_to_all(cell_buffer, 'tile', split_axis=0, co...  11.8 us
    max x24, other arithmetic, mark_step(): return jnp.maximum(depth, excess)  10.3 us
  transfers between devices with their start and end apart: 22, of which 14 were waited for; matrix products, arithmetic and copies ran while one was open for 17% of the time, Pallas kernels for 0%

commit v1 on v0

v1 whole, which is shorter than its diff:
```python
import functools

import jax
import jax.numpy as jnp
from jax import lax
from jax.experimental import pallas as pl
from jax.experimental.pallas import tpu as pltpu
from jax.sharding import PartitionSpec as P

MAXSTEP = 24
HEAT_STEPS = 4
SIGMA = 5.67e-08
BASE_KELVIN = 300.0
ZERO_CELSIUS = 273.15
LANE = 128
VMEM_LIMIT = 50 * 2**20

VMEM = pl.BlockSpec(memory_space=pltpu.VMEM)
SMEM = pl.BlockSpec(memory_space=pltpu.SMEM)


def split3(x):
    hi = x.astype(jnp.bfloat16)
    rest = x - hi.astype(jnp.float32)
    mid = rest.astype(jnp.bfloat16)
    low = (rest - mid.astype(jnp.float32)).astype(jnp.bfloat16)
    return hi, mid, low


def dot(a, b, dims):
    return lax.dot_general(a, b, (dims, ((), ())), preferred_element_type=jnp.float32)


def rank_records(tile_ref, tiles):
    count = tile_ref.shape[1]
    levels = lax.broadcasted_iota(jnp.int32, (tiles, count), 0)
    lane = lax.broadcasted_iota(jnp.int32, (tiles, count), 1)
    named = levels == tile_ref[...]
    running = named.astype(jnp.int32)
    step = 1
    while step < count:
        running = running + jnp.where(lane >= step, pltpu.roll(running, step, 1), 0)
        step *= 2
    ranking = jnp.sum(jnp.where(named, running - 1, 0), axis=0, keepdims=True)
    return named, ranking


def bucket_kernel(tiles, capacity, tile_ref, cell_ref, cells_ref):
    named, ranking = rank_records(tile_ref, tiles)
    slots = lax.broadcasted_iota(jnp.int32, (capacity, tile_ref.shape[1]), 0)
    chosen = (slots == ranking).astype(jnp.float32).astype(jnp.bfloat16)
    cell = cell_ref[...]
    parts = [
        jnp.where(named, ((cell >> (8 * p)) & 255).astype(jnp.float32), 0.0) for p in range(3)
    ]
    placed = dot(jnp.concatenate(parts, 0).astype(jnp.bfloat16), chosen, ((1,), (1,)))
    low, mid, high = (placed[p * tiles : (p + 1) * tiles].astype(jnp.int32) for p in range(3))
    cells_ref[...] = low + mid * 256 + high * 65536


def heat_kernel(suns, table_ref, sun_ref, anomaly_ref, class_ref, rows_ref, side_ref, view_ref, base_ref):
    row_count, col_count = class_ref.shape

    def assemble(own, i):
        left = jnp.concatenate([own, rows_ref[i]], 0)
        return jnp.concatenate([left, side_ref[i]], 1)

    mark = assemble((class_ref[...] + 1).astype(jnp.float32), 2)
    rates = [jnp.zeros_like(mark), jnp.zeros_like(mark)]
    for level in range(table_ref.shape[1]):
        here = mark == float(level + 1)
        rates = [jnp.where(here, table_ref[g, level], rates[g]) for g in range(2)]
    fourth = []
    for g in range(2):
        value = assemble(anomaly_ref[g], g)
        high, wide = value.shape
        for _ in range(HEAT_STEPS):
            beside = (
                pltpu.roll(value, 1, 0)
                + pltpu.roll(value, high - 1, 0)
                + pltpu.roll(value, 1, 1)
                + pltpu.roll(value, wide - 1, 1)
            )
            value = value + rates[g] * (beside - 4.0 * value)
        temp = BASE_KELVIN + value[:row_count, :col_count]
        temp = temp * temp
        fourth.append(SIGMA * temp * temp)
    sky = view_ref[0].astype(jnp.float32)
    wall = view_ref[1].astype(jnp.float32)
    reflected = view_ref[2].astype(jnp.float32) * wall
    emitted = 0.97 * (wall * fourth[1] + (1.0 - sky) * fourth[0])
    for s in range(suns):
        direct, diffuse, sky_long = sun_ref[s, 0], sun_ref[s, 1], sun_ref[s, 2]
        base_ref[s] = (
            emitted
            + sky * (0.7 * diffuse + 0.97 * sky_long)
            + reflected * (0.7 * (0.5 * direct + diffuse))
        )


def sun_kernel(
    geometry_ref, sun_ref, heights_ref, base_ref, cells_ref, out_ref, sampled_ref, field, parts
):
    slabs, ext_rows, slab_cols = heights_ref.shape
    row_count = base_ref.shape[1]
    cols = slabs * slab_cols
    window = row_count + MAXSTEP
    chunks = cols // LANE
    row_step, col_step = geometry_ref[0, 0], geometry_ref[0, 1]
    slope = 0.1 * geometry_ref[0, 2].astype(jnp.float32)
    steps = jnp.minimum(geometry_ref[0, 3], MAXSTEP)
    forward = row_step > 0
    first = pl.multiple_of(jnp.where(forward, MAXSTEP, 0), 8)
    own = pl.multiple_of(jnp.where(forward, 0, MAXSTEP), 8)

    zero = jnp.zeros((field.shape[1], LANE), jnp.float32)
    for a in range(2):
        field[a, :, 0:LANE] = zero
        field[a, :, LANE + cols : 2 * LANE + cols] = zero
    for j in range(slabs):
        begin = LANE + j * slab_cols
        field[0, 8 : 8 + window, begin : begin + slab_cols] = heights_ref[j, pl.ds(first, window), :]

    def shifted(a, chunk, begin, length, distance):
        down, move = row_step * distance, col_step * distance
        sub = lax.broadcasted_iota(jnp.int32, (length, LANE), 0) & 7
        lane = lax.broadcasted_iota(jnp.int32, (length, LANE), 1)
        same_rows = (sub >= jnp.maximum(down, 0)) & (sub < 8 + jnp.minimum(down, 0))
        same_cols = (lane >= jnp.maximum(move, 0)) & (lane < LANE + jnp.minimum(move, 0))
        at = pl.multiple_of((chunk + 1) * LANE, LANE)
        beyond = pl.multiple_of((chunk + 1 + col_step) * LANE, LANE)

        def across(start):
            rows = pl.ds(pl.multiple_of(start, 8), length)
            here, there = field[a, rows, pl.ds(at, LANE)], field[a, rows, pl.ds(beyond, LANE)]
            return jnp.where(same_cols, here, there)

        whole = jnp.where(same_rows, across(begin), across(begin + 8 * row_step))
        whole = whole.reshape(length // 8, 8, LANE)
        whole = pltpu.roll(whole, (8 - down) & 7, 1)
        return pltpu.roll(whole.reshape(length, LANE), (LANE - move) & (LANE - 1), 1)

    reached = jnp.int32(1)
    a = 0
    for _ in range(5):
        distance = jnp.clip(steps - reached, 0, reached)

        def stage(chunk, carry, a=a, distance=distance):
            at = pl.multiple_of((chunk + 1) * LANE, LANE)
            ahead = shifted(a, chunk, 8, window, distance) - slope * distance.astype(jnp.float32)
            here = field[a, 8 : 8 + window, pl.ds(at, LANE)]
            field[1 - a, 8 : 8 + window, pl.ds(at, LANE)] = jnp.maximum(here, ahead)
            return carry

        lax.fori_loop(0, chunks, stage, 0)
        reached = reached + distance
        a = 1 - a

    half_direct = 0.35 * sun_ref[0, 0]
    per_slab = slab_cols // LANE

    for slab in range(slabs):

        def finish(k, carry, slab=slab):
            chunk = slab * per_slab + k
            lanes = pl.ds(pl.multiple_of(k * LANE, LANE), LANE)
            centre = heights_ref[slab, MAXSTEP : MAXSTEP + row_count, lanes]
            depth = shifted(a, chunk, 8 + own, row_count, 1) - slope - centre
            depth = jnp.where(steps >= 1, depth, -100.0)
            sunlit = jnp.clip(0.5 - 0.5 * depth, 0.0, 1.0)
            absorbed = (base_ref[slab, :, lanes] + half_direct * sunlit) * (1.0 / (0.97 * SIGMA))
            value = jnp.sqrt(jnp.sqrt(absorbed)) - ZERO_CELSIUS
            at = pl.multiple_of(chunk * LANE, LANE)
            out_ref[0, :, pl.ds(at, LANE)] = value
            for p, part in enumerate(split3(value.T)):
                parts[pl.ds(at, LANE), p * row_count : (p + 1) * row_count] = part
            return carry

        lax.fori_loop(0, per_slab, finish, 0)

    group = cells_ref.shape[1]
    block = 256
    row_iota = lax.broadcasted_iota(jnp.int32, (row_count, group), 0)
    col_iota = lax.broadcasted_iota(jnp.int32, (block, group), 0)
    for g in range(cells_ref.shape[0]):
        cell = cells_ref[g : g + 1, :]
        pick = (row_iota == cell // cols).astype(jnp.float32).astype(jnp.bfloat16)
        pick = jnp.concatenate([pick] * 3, 0)
        col = cell % cols

        def gather(b, total, pick=pick, col=col):
            at = pl.multiple_of(b * block, block)
            rows = dot(parts[pl.ds(at, block), :], pick, ((1,), (0,)))
            return total + jnp.where(col_iota == col - at, rows, 0.0)

        total = lax.fori_loop(0, cols // block, gather, jnp.zeros((block, group), jnp.float32), unroll=4)
        sampled_ref[g : g + 1, :] = jnp.sum(total, axis=0, keepdims=True)


def excess_kernel(tiles, tile_ref, returned_ref, air_ref, excess_ref):
    named, ranking = rank_records(tile_ref, tiles)
    capacity = returned_ref.shape[1]
    slots = lax.broadcasted_iota(jnp.int32, (capacity, tile_ref.shape[1]), 0)
    chosen = (slots == ranking).astype(jnp.float32).astype(jnp.bfloat16)
    spread = sum(dot(part, chosen, ((1,), (0,))) for part in split3(returned_ref[...]))
    value = jnp.sum(jnp.where(named, spread, 0.0), axis=0, keepdims=True)
    excess_ref[...] = value - air_ref[...]


def call(kernel, out_shape, in_specs, scratch_shapes=()):
    out_specs = jax.tree.map(lambda _: VMEM, out_shape)
    return pl.pallas_call(
        kernel,
        out_shape=out_shape,
        in_specs=in_specs,
        out_specs=out_specs,
        scratch_shapes=scratch_shapes,
        compiler_params=pltpu.CompilerParams(vmem_limit_bytes=VMEM_LIMIT),
    )


def f32(*shape):
    return jax.ShapeDtypeStruct(shape, jnp.float32)


def exchange(axis, last, initial):
    peers = lax.axis_size(axis)
    up = [(i, (i + 1) % peers) for i in range(peers - 1)]
    down = [(j, i) for i, j in up]
    return lax.ppermute(last, axis, up), lax.ppermute(initial, axis, down)


def on_device(
    heights,
    classes,
    rate_table,
    anomaly,
    view_coef,
    sun_geometry,
    sun_radiation,
    record_tile,
    record_cell,
    record_air,
):
    row_count, col_count = heights.shape
    suns, tiles = lax.axis_size("sun"), lax.axis_size("tile")
    records = record_cell.shape[0]
    cols = suns * col_count
    capacity = 2 * records // tiles
    w = HEAT_STEPS

    target = record_tile.reshape(1, records)
    cells = call(
        functools.partial(bucket_kernel, tiles, capacity),
        jax.ShapeDtypeStruct((tiles, capacity), jnp.int32),
        [VMEM, VMEM],
    )(target, record_cell.reshape(1, records))
    cells = lax.all_to_all(cells, "tile", split_axis=0, concat_axis=0, tiled=True)

    mark = (classes + 1).astype(jnp.float32)

    def edge(lo, hi, hlo, hhi):
        return jnp.concatenate(
            [anomaly[0, lo:hi], anomaly[1, lo:hi], mark[lo:hi], heights[hlo:hhi]], 0
        )

    before, after = exchange(
        "tile",
        edge(row_count - w, row_count, row_count - MAXSTEP, row_count),
        edge(0, w, 0, MAXSTEP),
    )
    rows = jnp.stack(
        [jnp.concatenate([after[i * w : (i + 1) * w], before[i * w : (i + 1) * w]], 0) for i in range(3)]
    )
    heights_ext = jnp.concatenate([before[3 * w :], heights, after[3 * w :]], 0)
    heights_all = lax.all_gather(heights_ext, "sun", axis=0)

    fields = jnp.concatenate([anomaly, mark[None]], 0)

    def column(lo, hi):
        return jnp.concatenate([fields[:, :, lo:hi], rows[:, :, lo:hi]], 1)

    left, right = exchange("sun", column(col_count - w, col_count), column(0, w))
    side = jnp.concatenate(
        [right, jnp.zeros((3, row_count + 2 * w, LANE - 2 * w), jnp.float32), left], 2
    )
    radiation_all = lax.all_gather(sun_radiation[0], "sun", axis=0)
    base = call(
        functools.partial(heat_kernel, suns),
        f32(suns, row_count, col_count),
        [SMEM, SMEM] + [VMEM] * 5,
    )(rate_table, radiation_all, anomaly, classes, rows, side, view_coef)
    base = lax.all_to_all(base, "sun", split_axis=0, concat_axis=0, tiled=True)

    group = 256
    window = row_count + MAXSTEP
    radiant_block, sampled = call(
        sun_kernel,
        (f32(1, row_count, cols), f32(tiles * capacity // group, group)),
        [SMEM, SMEM] + [VMEM] * 3,
        [
            pltpu.VMEM((2, window + 16, cols + 2 * LANE), jnp.float32),
            pltpu.VMEM((cols, 3 * row_count), jnp.bfloat16),
        ],
    )(sun_geometry, sun_radiation, heights_all, base, cells.reshape(-1, group))
    returned = lax.all_to_all(
        sampled.reshape(tiles, capacity), "tile", split_axis=0, concat_axis=0, tiled=True
    )
    excess = call(functools.partial(excess_kernel, tiles), f32(1, records), [VMEM] * 3)(
        target, returned, record_air.reshape(1, records)
    )
    return radiant_block, excess.reshape(records)


def solution(mesh):
    return jax.shard_map(
        on_device,
        mesh=mesh,
        in_specs=(
            P("tile", "sun"),
            P("tile", "sun"),
            P(),
            P(None, "tile", "sun"),
            P(None, "tile", "sun"),
            P("sun", None),
            P("sun", None),
            P(("tile", "sun"), None),
            P(("tile", "sun")),
            P(("tile", "sun")),
        ),
        out_specs=(P("sun", "tile", None), P(("tile", "sun"))),
        check_vma=False,
    )
```

time: 244 us -> 79.5 us (0.33)
  loops' own time: 45.1 us -> 0 us
  waiting for transfers between devices: 42.8 us -> 0.89 us
  local copies, waits for them, and re-layouts: 42.7 us -> 5.21 us
  other arithmetic: 36 us -> 1.05 us
  starting transfers between devices: 46.4 us -> 21.6 us
  blocking collectives: 9.62 us -> 33.9 us
  between operations: 16.3 us -> 0.89 us
  Pallas kernels: 0 us -> 15.3 us
  matrix products: 3.81 us -> 0 us
    another operation x1 -> x0, loops' own time: 45.1 us -> none  [sunlit_share(): lax.fori_loop(1, MAXSTEP + 1, mark_step, jnp.full((row_count, col_count),...]
    ppermute x18 -> x4, waiting for transfers between devices: 34.1 us -> 0.88 us  [exchange(): return (lax.ppermute(last, axis, up), lax.ppermute(initial, axis, down))]
    ppermute x18 -> x4, starting transfers between devices: 33.6 us -> 10.3 us  [exchange(): return (lax.ppermute(last, axis, up), lax.ppermute(initial, axis, down))]
    gather x2 -> x0, local copies, waits for them, and re-layouts: 17.9 us -> none  [the longest x1 11.8 us: on_device(): jnp.take(flat_block, lax.all_to_all(cell_buffer, 'tile', split_axis=0, co...]
    slice x32 -> x7, local copies, waits for them, and re-layouts: 16.3 us -> 0.94 us  [the longest x1 0.83 us: edge(): heights[hlo:hhi]]
    pallas_call x0 -> x4, Pallas kernels: none -> 15.3 us  [the longest x1 8.8 us: on_device(): call(sun_kernel, (f32(1, row_count, cols), f32(tiles * capacity // group,...]
    all_gather x1 -> x2, blocking collectives: 9.62 us -> 21.8 us  [the longest x1 17.2 us: on_device(): heights_all = lax.all_gather(heights_ext, 'sun', axis=0)]
    all_to_all x0 -> x1, blocking collectives: none -> 12.1 us  [on_device(): lax.all_to_all(sampled.reshape(tiles, capacity), 'tile', split_axis=0, co...]
  transfers between devices with their start and end apart: 22 -> 6, of which waited for: 14 -> 1; matrix products, arithmetic and copies ran while one was open for 17% -> 4% of each run, Pallas kernels for 0% -> 0%
where the time goes in v1:
time: 79.5 us; the launch traced here: 78.9 us
  blocking collectives  33.9 us (43%)
  starting transfers between devices  21.6 us (27%)
  Pallas kernels  15.3 us (19%)
  local copies, waits for them, and re-layouts  5.21 us (7%)
  other arithmetic  1.05 us (1%)
  waiting for transfers between devices  0.89 us (1%)
  between operations  0.89 us (1%)
    all_gather x1, blocking collectives, on_device(): heights_all = lax.all_gather(heights_ext, 'sun', axis=0)  17.2 us
    all_to_all x1, blocking collectives, on_device(): lax.all_to_all(sampled.reshape(tiles, capacity), 'tile', split_axis=0, co...  12.1 us
    ppermute x4, starting transfers between devices, exchange(): return (lax.ppermute(last, axis, up), lax.ppermute(initial, axis, down))  10.3 us
    pallas_call x1, Pallas kernels, on_device(): call(sun_kernel, (f32(1, row_count, cols), f32(tiles * capacity // group,...  8.8 us
    all_to_all x1, starting transfers between devices, on_device(): lax.all_to_all(cells, 'tile', split_axis=0, concat_axis=0, tiled=True)  7.39 us
    all_gather x1, blocking collectives, on_device(): radiation_all = lax.all_gather(sun_radiation[0], 'sun', axis=0)  4.62 us
    all_to_all x1, starting transfers between devices, on_device(): base = lax.all_to_all(base, 'sun', split_axis=0, concat_axis=0, tiled=True)  3.9 us
    pallas_call x1, Pallas kernels, on_device(): call(functools.partial(heat_kernel, suns), f32(suns, row_count, col_count...  3.73 us
  transfers between devices with their start and end apart: 6, of which 1 were waited for; matrix products, arithmetic and copies ran while one was open for 4% of the time, Pallas kernels for 0%

profile of v1, /device:TPU:0, one launch (start us, length us, event | category | flops | bytes accessed | tf_op | source)
XLA Modules:
  0.0 78.9 jit_solution(2688480023831331324)
XLA Ops:
  0.6 0.0 copy-start.3
  0.7 0.7 copy-done.3
  1.4 0.7 copy-done.6
  2.1 1.4 %shard_map.114 = s32[16,128]{1,0:T(8,128)} custom-call(s32[1,1024]{1,0:T(1,128)S(1)} %bitcast.30, s32[1,1024]{1,0:T(1,128)S(1)} %bitcast.33), custom_call_target="tpu_custom_call" | custom-call | tf_op jit(solution)/shard_map/pallas_call | solution.py:253
  3.4 7.4 %all-to-all-start.1 = ((s32[16,1,128]{2,1,0:T(1,128)}), s32[16,1,128]{2,1,0:T(1,128)S(1)}, u32[]{:S(2)}, u32[]{:S(2)}) async-start(s32[16,1,128]{2,1,0:T(1,128)} %bitcast.14), calls=%async_computation.1 | async-start | bytes 16384 | tf_op jit(solution)/shard_map/all_to_all | solution.py:258
  10.8 0.8 slice_bitcast_fusion.3
  11.6 0.8 %fusion.4 = (f32[24,512]{1,0:T(8,128)S(1)}, f32[24,512]{1,0:T(8,128)S(1)}) fusion(f32[128,512]{1,0:T(8,128)} %param.10), kind=kLoop, calls=%fused_computation.19 | loop fusion | bytes 196608 | tf_op jit(solution)/shard_map/slice | solution.py:264
  12.5 0.1 fusion.2
  12.5 0.0 copy-start
  12.6 1.4 %collective-permute-start.1 = (f32[36,512]{1,0:T(8,128)S(1)}, f32[36,512]{1,0:T(8,128)S(1)}, u32[]{:S(2)}, u32[]{:S(2)}) collective-permute-start(f32[36,512]{1,0:T(8,128)S(1)} %pad_maximum_fusion.5), channel_id=1, source_target_pairs={{2,0},{4,2},{6,4},{8,6},{10,8},{12,10},{14,12},{16,14},{18,16},{20... | collective-permute-start | bytes 221192 | tf_op jit(solution)/shard_map/ppermute | solution.py:230
  14.0 3.0 %collective-permute-start = (f32[36,512]{1,0:T(8,128)S(1)}, f32[36,512]{1,0:T(8,128)S(1)}, u32[]{:S(2)}, u32[]{:S(2)}) collective-permute-start(f32[36,512]{1,0:T(8,128)S(1)} %pad_maximum_fusion.4), channel_id=1, source_target_pairs={{0,2},{2,4},{4,6},{6,8},{8,10},{10,12},{12,14},{14,16},{16,18},{18... | collective-permute-start | bytes 221192 | tf_op jit(solution)/shard_map/ppermute | solution.py:230
  17.1 0.9 %collective-permute-done = f32[36,512]{1,0:T(8,128)S(1)} collective-permute-done((f32[36,512]{1,0:T(8,128)S(1)}, f32[36,512]{1,0:T(8,128)S(1)}, u32[]{:S(2)}, u32[]{:S(2)}) %collective-permute-start) | collective-permute-done | bytes 73760 | tf_op jit(solution)/shard_map/ppermute | solution.py:230
  18.0 0.1 fusion.7
  18.1 0.1 fusion.1
  18.2 1.3 %collective-permute-start.2 = (f32[3,136,4]{2,1,0:T(8,128)S(1)}, f32[3,136,4]{2,1,0:T(8,128)S(1)}, u32[]{:S(2)}, u32[]{:S(2)}) collective-permute-start(f32[3,136,4]{2,1,0:T(8,128)S(1)} %get-tuple-element.6), channel_id=1, source_target_pairs={{1,0},{3,2},{5,4},{7,6},{9,8},{11,10},{13,12},{15,14},{17,16},{19,... | collective-permute-start | bytes 19592 | tf_op jit(solution)/shard_map/ppermute | solution.py:230
  19.5 0.0 copy-start.9
  19.5 4.6 %collective-permute-start.3 = (f32[3,136,4]{2,1,0:T(8,128)S(1)}, f32[3,136,4]{2,1,0:T(8,128)S(1)}, u32[]{:S(2)}, u32[]{:S(2)}) collective-permute-start(f32[3,136,4]{2,1,0:T(8,128)S(1)} %get-tuple-element.7), channel_id=1, source_target_pairs={{0,1},{2,3},{4,5},{6,7},{8,9},{10,11},{12,13},{14,15},{16,17},{18,... | collective-permute-start | bytes 19592 | tf_op jit(solution)/shard_map/ppermute | solution.py:230
  24.1 4.6 %all-gather.1 = f32[2,1,3]{2,1,0:T(1,128)S(1)} all-gather(f32[1,1,3]{2,1,0:T(1,128)S(1)} %bitcast.35), channel_id=1, replica_groups=mesh['tile'=16,'sun'=2] {'sun'}, dimensions={0}, use_global_device_ids=true | all-gather | bytes 36 | tf_op jit(solution)/shard_map/all_gather | solution.py:287
  28.7 0.1 pad.1.clone
  28.8 0.5 broadcast.5
  29.3 0.7 reduce.3
  30.1 0.1 pad_maximum_fusion.3.side_ref
  30.2 0.8 %copy-done.2 = bf16[3,128,512]{2,1,0:T(8,128)(2,1)S(1)} copy-done((bf16[3,128,512]{2,1,0:T(8,128)(2,1)S(1)}, bf16[3,128,512]{2,1,0:T(8,128)(2,1)}, u32[]{:S(2)}) %copy-start.2) | copy-done | bytes 393240
  31.0 3.7 %shard_map.113 = f32[2,128,512]{2,1,0:T(8,128)} custom-call(f32[2,16]{1,0:T(2,128)S(1)} %copy-done.7, f32[2,3]{1,0:T(2,128)S(1)} %bitcast.34, f32[2,128,512]{2,1,0:T(8,128)S(1)} %copy-done, s32[128,512]{1,0:T(8,128)S(1)} %copy-done.1, f32[3,8,512]{2,1,0:T(8,128)S(1)} %pad_maximum_fusion.6.rows_ref, f32[3,136,128]{2,1,0:T(8,128)S(1)} %pad_maximum_fusion.3.side_ref, ...), custom_call_target="tpu_custom_call" | custom-call | tf_op jit(solution)/shard_map/pallas_call | solution.py:288
  34.8 3.9 %all-to-all-start = ((f32[2,128,512]{2,1,0:T(8,128)}), f32[2,128,512]{2,1,0:T(8,128)S(1)}, u32[]{:S(2)}, u32[]{:S(2)}) async-start(f32[2,128,512]{2,1,0:T(8,128)} %shard_map.113), calls=%async_computation | async-start | bytes 1048576 | tf_op jit(solution)/shard_map/all_to_all | solution.py:293
  38.7 17.2 %all-gather = f32[352,512]{1,0:T(8,128)S(1)} all-gather(f32[176,512]{1,0:T(8,128)S(1)} %pad_maximum_fusion), channel_id=2, replica_groups=mesh['tile'=16,'sun'=2] {'sun'}, dimensions={0}, use_global_device_ids=true | all-gather | bytes 1081344 | tf_op jit(solution)/shard_map/all_gather | solution.py:276
  55.9 0.7 copy-done.8
  56.5 8.8 %shard_map.115 = (f32[1,128,1024]{2,1,0:T(8,128)}, f32[8,256]{1,0:T(8,128)S(1)}) custom-call(s32[1,4]{1,0:T(1,128)S(1)} %copy-done.8, f32[1,3]{1,0:T(1,128)S(1)} %copy-done.9, f32[2,176,512]{2,1,0:T(8,128)S(1)} %bitcast.28, f32[2,128,512]{2,1,0:T(8,128)S(1)} %all-to-all-done.base_ref, s32[8,256]{1,0:T(8,128)S(1)} %reshape.28.cells_ref), custom_call_target="tpu_custom_call" | custom-call | tf_op jit(solution)/shard_map/pallas_call | solution.py:297
  65.4 0.0 copy-start.4
  65.4 0.0 copy-start.5
  65.4 12.1 %all_to_all.25 = f32[16,1,128]{2,1,0:T(1,128)S(1)} all-to-all(f32[16,1,128]{2,1,0:T(1,128)S(1)} %bitcast.36), channel_id=1, replica_groups=mesh['tile'=16,'sun'=2] {'tile'}, dimensions={0} | all-to-all | bytes 16384 | tf_op jit(solution)/shard_map/all_to_all | solution.py:306
  77.5 1.4 %shard_map.116 = f32[1,1024]{1,0:T(1,128)} custom-call(s32[1,1024]{1,0:T(1,128)S(1)} %bitcast.31, f32[16,128]{1,0:T(8,128)S(1)} %bitcast.29, f32[1,1024]{1,0:T(1,128)S(1)} %bitcast.32), custom_call_target="tpu_custom_call" | custom-call | tf_op jit(solution)/shard_map/pallas_call | solution.py:309
  (32 shorter events, 0.2 us)
Async XLA Ops:
  0.6 11.8 %copy-start.1 = (s32[128,512]{1,0:T(8,128)S(1)}, s32[128,512]{1,0:T(8,128)}, u32[]{:S(2)}) copy-start(s32[128,512]{1,0:T(8,128)} %class_ref.1) | copy-start | bytes 786436
  0.6 0.7 copy-start.3
  1.4 0.7 copy-start.6
  3.4 25.4 %all-to-all-start.1 = ((s32[16,1,128]{2,1,0:T(1,128)}), s32[16,1,128]{2,1,0:T(1,128)S(1)}, u32[]{:S(2)}, u32[]{:S(2)}) async-start(s32[16,1,128]{2,1,0:T(1,128)} %bitcast.14), calls=%async_computation.1 | async-start | bytes 16384 | tf_op jit(solution)/shard_map/all_to_all | solution.py:258
  12.5 5.6 %copy-start = (f32[2,128,512]{2,1,0:T(8,128)S(1)}, f32[2,128,512]{2,1,0:T(8,128)}, u32[]{:S(2)}) copy-start(f32[2,128,512]{2,1,0:T(8,128)} %anomaly_ref.1) | copy-start | bytes 1572868
  12.6 4.5 %collective-permute-start.1 = (f32[36,512]{1,0:T(8,128)S(1)}, f32[36,512]{1,0:T(8,128)S(1)}, u32[]{:S(2)}, u32[]{:S(2)}) collective-permute-start(f32[36,512]{1,0:T(8,128)S(1)} %pad_maximum_fusion.5), channel_id=1, source_target_pairs={{2,0},{4,2},{6,4},{8,6},{10,8},{12,10},{14,12},{16,14},{18,16},{20... | collective-permute-start | bytes 221192 | tf_op jit(solution)/shard_map/ppermute | solution.py:230
  14.0 3.9 %collective-permute-start = (f32[36,512]{1,0:T(8,128)S(1)}, f32[36,512]{1,0:T(8,128)S(1)}, u32[]{:S(2)}, u32[]{:S(2)}) collective-permute-start(f32[36,512]{1,0:T(8,128)S(1)} %pad_maximum_fusion.4), channel_id=1, source_target_pairs={{0,2},{2,4},{4,6},{6,8},{8,10},{10,12},{12,14},{14,16},{16,18},{18... | collective-permute-start | bytes 221192 | tf_op jit(solution)/shard_map/ppermute | solution.py:230
  18.2 11.8 %collective-permute-start.2 = (f32[3,136,4]{2,1,0:T(8,128)S(1)}, f32[3,136,4]{2,1,0:T(8,128)S(1)}, u32[]{:S(2)}, u32[]{:S(2)}) collective-permute-start(f32[3,136,4]{2,1,0:T(8,128)S(1)} %get-tuple-element.6), channel_id=1, source_target_pairs={{1,0},{3,2},{5,4},{7,6},{9,8},{11,10},{13,12},{15,14},{17,16},{19,... | collective-permute-start | bytes 19592 | tf_op jit(solution)/shard_map/ppermute | solution.py:230
  19.5 4.6 %copy-start.9 = (f32[1,3]{1,0:T(1,128)S(1)}, f32[1,3]{1,0:T(1,128)}, u32[]{:S(2)}) copy-start(f32[1,3]{1,0:T(1,128)} %sun_ref.1) | copy-start | bytes 40
  19.5 10.5 %collective-permute-start.3 = (f32[3,136,4]{2,1,0:T(8,128)S(1)}, f32[3,136,4]{2,1,0:T(8,128)S(1)}, u32[]{:S(2)}, u32[]{:S(2)}) collective-permute-start(f32[3,136,4]{2,1,0:T(8,128)S(1)} %get-tuple-element.7), channel_id=1, source_target_pairs={{0,1},{2,3},{4,5},{6,7},{8,9},{10,11},{12,13},{14,15},{16,17},{18,... | collective-permute-start | bytes 19592 | tf_op jit(solution)/shard_map/ppermute | solution.py:230
  30.0 1.0 %copy-start.2 = (bf16[3,128,512]{2,1,0:T(8,128)(2,1)S(1)}, bf16[3,128,512]{2,1,0:T(8,128)(2,1)}, u32[]{:S(2)}) copy-start(bf16[3,128,512]{2,1,0:T(8,128)(2,1)} %view_ref.1) | copy-start | bytes 1179652
  30.2 0.8 %copy-start.7 = (f32[2,16]{1,0:T(2,128)S(1)}, f32[2,16]{1,0:T(2,128)}, u32[]{:S(2)}) copy-start(f32[2,16]{1,0:T(2,128)} %table_ref.1) | copy-start | bytes 388
  34.7 3.9 %copy-start.10 = (f32[128,512]{1,0:T(8,128)S(1)}, f32[128,512]{1,0:T(8,128)}, u32[]{:S(2)}) copy-start(f32[128,512]{1,0:T(8,128)} %param.10) | copy-start | bytes 786436
  34.8 21.1 %all-to-all-start = ((f32[2,128,512]{2,1,0:T(8,128)}), f32[2,128,512]{2,1,0:T(8,128)S(1)}, u32[]{:S(2)}, u32[]{:S(2)}) async-start(f32[2,128,512]{2,1,0:T(8,128)} %shard_map.113), calls=%async_computation | async-start | bytes 1048576 | tf_op jit(solution)/shard_map/all_to_all | solution.py:293
  55.9 0.7 copy-start.8
  65.4 12.1 %copy-start.4 = (s32[1024,1]{0,1:T(1,128)S(1)}, s32[1024,1]{0,1:T(1,128)}, u32[]{:S(2)}) copy-start(s32[1024,1]{0,1:T(1,128)} %param.17) | copy-start | bytes 12292
  65.4 12.1 %copy-start.5 = (f32[1024]{0:T(1024)S(1)}, f32[1024]{0:T(1024)}, u32[]{:S(2)}) copy-start(f32[1024]{0:T(1024)} %param.19) | copy-start | bytes 12292

commit v2 on v1

--- a/solution.py
+++ b/solution.py
@@ -45,41 +45,166 @@
     return named, ranking
 
 
-def bucket_kernel(tiles, capacity, tile_ref, cell_ref, cells_ref):
+def bucket(tiles, capacity, tile_ref, cell_ref):
     named, ranking = rank_records(tile_ref, tiles)
     slots = lax.broadcasted_iota(jnp.int32, (capacity, tile_ref.shape[1]), 0)
     chosen = (slots == ranking).astype(jnp.float32).astype(jnp.bfloat16)
     cell = cell_ref[...]
-    parts = [
+    pieces = [
         jnp.where(named, ((cell >> (8 * p)) & 255).astype(jnp.float32), 0.0) for p in range(3)
     ]
-    placed = dot(jnp.concatenate(parts, 0).astype(jnp.bfloat16), chosen, ((1,), (1,)))
+    placed = dot(jnp.concatenate(pieces, 0).astype(jnp.bfloat16), chosen, ((1,), (1,)))
     low, mid, high = (placed[p * tiles : (p + 1) * tiles].astype(jnp.int32) for p in range(3))
-    cells_ref[...] = low + mid * 256 + high * 65536
-
-
-def heat_kernel(suns, table_ref, sun_ref, anomaly_ref, class_ref, rows_ref, side_ref, view_ref, base_ref):
+    return low + mid * 256 + high * 65536
+
+
+def remote(src, dst, sems, k, tile, sun):
+    return pltpu.make_async_remote_copy(
+        src_ref=src,
+        dst_ref=dst,
+        send_sem=sems.at[0, k],
+        recv_sem=sems.at[1, k],
+        device_id=(tile, sun),
+        device_id_type=pl.DeviceIdType.MESH,
+    )
+
+
+def greet(peers):
+    barrier = pltpu.get_barrier_semaphore()
+    for peer in peers:
+        pl.semaphore_signal(
+            barrier, inc=1, device_id=peer, device_id_type=pl.DeviceIdType.MESH
+        )
+    pl.semaphore_wait(barrier, len(peers))
+
+
+def heat_kernel(
+    tiles, suns, table_ref, sun_ref, heights_ref, anomaly_ref, class_ref, view_ref, tile_ref, cell_ref,
+    heights_all, base_all, cells_in,
+    fields, rows_in, cols_out, cols_in, corners_in, light_out, light_in, base_out, cells_out,
+    near_sems, light_sems, cell_sems, height_sems, base_sems,
+):
     row_count, col_count = class_ref.shape
-
-    def assemble(own, i):
-        left = jnp.concatenate([own, rows_ref[i]], 0)
-        return jnp.concatenate([left, side_ref[i]], 1)
-
-    mark = assemble((class_ref[...] + 1).astype(jnp.float32), 2)
+    capacity = cells_in.shape[2]
+    tile, sun = lax.axis_index("tile"), lax.axis_index("sun")
+    above, below = lax.rem(tile + tiles - 1, tiles), lax.rem(tile + 1, tiles)
+    before, after = lax.rem(sun + suns - 1, suns), lax.rem(sun + 1, suns)
+    other_tiles = [lax.rem(tile + k, tiles) for k in range(1, tiles)]
+    other_suns = [lax.rem(sun + k, suns) for k in range(1, suns)]
+
+    fields[0] = anomaly_ref[0]
+    fields[1] = anomaly_ref[1]
+    fields[2] = (class_ref[...] + 1).astype(jnp.float32)
+    last = col_count - LANE
+    for i in range(3):
+        cols_out[0, i] = fields[i, :, 0:LANE].T[0:8]
+        cols_out[1, i] = fields[i, :, last:col_count].T[LANE - 8 : LANE]
+    lane = lax.broadcasted_iota(jnp.int32, (1, LANE), 1)
+    light = jnp.zeros((1, LANE), jnp.float32)
+    for i in range(3):
+        light = jnp.where(lane == i, sun_ref[0, i], light)
+    light_out[...] = light
+    light_in[sun] = light
+
+    greet(
+        [(t, sun) for t in other_tiles]
+        + [(t, s) for s in other_suns for t in (above, tile, below)]
+    )
+    top, bottom = pl.ds(0, 8), pl.ds(row_count - 8, 8)
+    first_cols, last_cols = pl.ds(0, LANE), pl.ds(last, LANE)
+    near = [
+        remote(cols_out.at[0], cols_in.at[1], near_sems, 0, tile, before),
+        remote(cols_out.at[1], cols_in.at[0], near_sems, 1, tile, after),
+        remote(fields.at[:, top, :], rows_in.at[0], near_sems, 2, above, sun),
+        remote(fields.at[:, bottom, :], rows_in.at[1], near_sems, 3, below, sun),
+        remote(fields.at[:, top, first_cols], corners_in.at[0, 1], near_sems, 4, above, before),
+        remote(fields.at[:, top, last_cols], corners_in.at[0, 0], near_sems, 5, above, after),
+        remote(fields.at[:, bottom, first_cols], corners_in.at[1, 1], near_sems, 6, below, before),
+        remote(fields.at[:, bottom, last_cols], corners_in.at[1, 0], near_sems, 7, below, after),
+    ] + [
+        remote(light_out, light_in.at[sun], light_sems, k, tile, s)
+        for k, s in enumerate(other_suns)
+    ]
+    for copy in near:
+        copy.start()
+    far = []
+    for k, s in enumerate(other_suns):
+        far.append(
+            remote(heights_ref, heights_all.at[sun, pl.ds(MAXSTEP, row_count), :], height_sems, k, tile, s)
+        )
+    for k, s in enumerate([sun] + other_suns):
+        at = suns - 1 + 2 * k
+        far.append(
+            remote(
+                heights_ref.at[pl.ds(0, MAXSTEP), :],
+                heights_all.at[sun, pl.ds(MAXSTEP + row_count, MAXSTEP), :],
+                height_sems, at, above, s,
+            )
+        )
+        far.append(
+            remote(
+                heights_ref.at[pl.ds(row_count - MAXSTEP, MAXSTEP), :],
+                heights_all.at[sun, pl.ds(0, MAXSTEP), :],
+                height_sems, at + 1, below, s,
+            )
+        )
+    for copy in far:
+        copy.start()
+    heights_all[sun, MAXSTEP : MAXSTEP + row_count, :] = heights_ref[...]
+
+    cells = bucket(tiles, capacity, tile_ref, cell_ref)
+    for t in range(tiles):
+        cells_out[t] = cells[t : t + 1]
+    cells_in[tile] = cells_out[tile]
+    for k, t in enumerate(other_tiles):
+        copy = remote(cells_out.at[t], cells_in.at[tile], cell_sems, k, t, sun)
+        copy.start()
+        far.append(copy)
+
+    for copy in near:
+        copy.wait_recv()
+    has_above, has_below = tile > 0, tile < tiles - 1
+    has_before, has_after = sun > 0, sun < suns - 1
+    wide = lax.broadcasted_iota(jnp.int32, (8, LANE), 1)
+
+    def masked(condition, value):
+        return jnp.where(condition, value, 0.0)
+
+    def corner(k, i, present):
+        left = masked(present & has_before, corners_in[k, 0, i])
+        right = masked(present & has_after, corners_in[k, 1, i])
+        return jnp.where(wide < LANE // 2, right, left)
+
+    def assemble(i):
+        own = jnp.concatenate(
+            [fields[i], masked(has_below, rows_in[0, i]), masked(has_above, rows_in[1, i])], 0
+        )
+        flat = jnp.concatenate(
+            [
+                masked(has_after, cols_in[1, i]),
+                jnp.zeros((LANE - 16, row_count), jnp.float32),
+                masked(has_before, cols_in[0, i]),
+            ],
+            0,
+        )
+        side = jnp.concatenate([flat.T, corner(0, i, has_below), corner(1, i, has_above)], 0)
+        return jnp.concatenate([own, side], 1)
+
+    mark = assemble(2)
     rates = [jnp.zeros_like(mark), jnp.zeros_like(mark)]
     for level in range(table_ref.shape[1]):
         here = mark == float(level + 1)
         rates = [jnp.where(here, table_ref[g, level], rates[g]) for g in range(2)]
     fourth = []
     for g in range(2):
-        value = assemble(anomaly_ref[g], g)
-        high, wide = value.shape
+        value = assemble(g)
+        high, broad = value.shape
         for _ in range(HEAT_STEPS):
             beside = (
                 pltpu.roll(value, 1, 0)
                 + pltpu.roll(value, high - 1, 0)
                 + pltpu.roll(value, 1, 1)
-                + pltpu.roll(value, wide - 1, 1)
+                + pltpu.roll(value, broad - 1, 1)
             )
             value = value + rates[g] * (beside - 4.0 * value)
         temp = BASE_KELVIN + value[:row_count, :col_count]
@@ -90,12 +215,32 @@
     reflected = view_ref[2].astype(jnp.float32) * wall
     emitted = 0.97 * (wall * fourth[1] + (1.0 - sky) * fourth[0])
     for s in range(suns):
-        direct, diffuse, sky_long = sun_ref[s, 0], sun_ref[s, 1], sun_ref[s, 2]
-        base_ref[s] = (
+        received = light_in[s]
+        direct, diffuse, sky_long = received[:, 0:1], received[:, 1:2], received[:, 2:3]
+        base_out[s] = (
             emitted
             + sky * (0.7 * diffuse + 0.97 * sky_long)
             + reflected * (0.7 * (0.5 * direct + diffuse))
         )
+    for k, s in enumerate(other_suns):
+        copy = remote(base_out.at[s], base_all.at[sun], base_sems, k, tile, s)
+        copy.start()
+        far.append(copy)
+    base_all[sun] = base_out[sun]
+    for copy in far:
+        copy.wait_recv()
+    edge = jnp.zeros((suns, MAXSTEP, col_count), jnp.float32)
+
+    @pl.when(tile == 0)
+    def _():
+        heights_all[:, 0:MAXSTEP, :] = edge
+
+    @pl.when(tile == tiles - 1)
+    def _():
+        heights_all[:, MAXSTEP + row_count : 2 * MAXSTEP + row_count, :] = edge
+
+    for copy in near + far:
+        copy.wait_send()
 
 
 def sun_kernel(
@@ -178,12 +323,13 @@
 
         lax.fori_loop(0, per_slab, finish, 0)
 
-    group = cells_ref.shape[1]
+    capacity = cells_ref.shape[2]
+    group = 2 * capacity
     block = 256
     row_iota = lax.broadcasted_iota(jnp.int32, (row_count, group), 0)
     col_iota = lax.broadcasted_iota(jnp.int32, (block, group), 0)
-    for g in range(cells_ref.shape[0]):
-        cell = cells_ref[g : g + 1, :]
+    for g in range(cells_ref.shape[0] // 2):
+        cell = jnp.concatenate([cells_ref[2 * g], cells_ref[2 * g + 1]], 1)
         pick = (row_iota == cell // cols).astype(jnp.float32).astype(jnp.bfloat16)
         pick = jnp.concatenate([pick] * 3, 0)
         col = cell % cols
@@ -194,40 +340,50 @@
             return total + jnp.where(col_iota == col - at, rows, 0.0)
 
         total = lax.fori_loop(0, cols // block, gather, jnp.zeros((block, group), jnp.float32), unroll=4)
-        sampled_ref[g : g + 1, :] = jnp.sum(total, axis=0, keepdims=True)
-
-
-def excess_kernel(tiles, tile_ref, returned_ref, air_ref, excess_ref):
+        total = jnp.sum(total, axis=0, keepdims=True)
+        sampled_ref[2 * g] = total[:, :capacity]
+        sampled_ref[2 * g + 1] = total[:, capacity:]
+
+
+def excess_kernel(tiles, suns, tile_ref, sampled_ref, air_ref, excess_ref, returned, sems):
+    tile, sun = lax.axis_index("tile"), lax.axis_index("sun")
+    others = [lax.rem(tile + k, tiles) for k in range(1, tiles)]
+    greet([(t, sun) for t in others])
+    copies = [
+        remote(sampled_ref.at[t], returned.at[tile], sems, k, t, sun) for k, t in enumerate(others)
+    ]
+    for copy in copies:
+        copy.start()
+    returned[tile] = sampled_ref[tile]
     named, ranking = rank_records(tile_ref, tiles)
-    capacity = returned_ref.shape[1]
+    capacity = returned.shape[2]
     slots = lax.broadcasted_iota(jnp.int32, (capacity, tile_ref.shape[1]), 0)
     chosen = (slots == ranking).astype(jnp.float32).astype(jnp.bfloat16)
-    spread = sum(dot(part, chosen, ((1,), (0,))) for part in split3(returned_ref[...]))
+    for copy in copies:
+        copy.wait()
+    values = jnp.concatenate([returned[t] for t in range(tiles)], 0)
+    spread = sum(dot(part, chosen, ((1,), (0,))) for part in split3(values))
     value = jnp.sum(jnp.where(named, spread, 0.0), axis=0, keepdims=True)
     excess_ref[...] = value - air_ref[...]
 
 
-def call(kernel, out_shape, in_specs, scratch_shapes=()):
+def call(kernel, out_shape, in_specs, scratch_shapes=(), collective_id=None):
     out_specs = jax.tree.map(lambda _: VMEM, out_shape)
+    sends = collective_id is not None
     return pl.pallas_call(
         kernel,
         out_shape=out_shape,
         in_specs=in_specs,
         out_specs=out_specs,
         scratch_shapes=scratch_shapes,
-        compiler_params=pltpu.CompilerParams(vmem_limit_bytes=VMEM_LIMIT),
+        compiler_params=pltpu.CompilerParams(
+            vmem_limit_bytes=VMEM_LIMIT, collective_id=collective_id, has_side_effects=sends
+        ),
     )
 
 
 def f32(*shape):
     return jax.ShapeDtypeStruct(shape, jnp.float32)
-
-
-def exchange(axis, last, initial):
-    peers = lax.axis_size(axis)
-    up = [(i, (i + 1) % peers) for i in range(peers - 1)]
-    down = [(j, i) for i, j in up]
-    return lax.ppermute(last, axis, up), lax.ppermute(initial, axis, down)
 
 
 def on_device(
@@ -246,69 +402,67 @@
     suns, tiles = lax.axis_size("sun"), lax.axis_size("tile")
     records = record_cell.shape[0]
     cols = suns * col_count
-    capacity = 2 * records // tiles
-    w = HEAT_STEPS
-
+    capacity = -(-2 * records // tiles // LANE) * LANE
+    window = row_count + MAXSTEP
     target = record_tile.reshape(1, records)
-    cells = call(
-        functools.partial(bucket_kernel, tiles, capacity),
-        jax.ShapeDtypeStruct((tiles, capacity), jnp.int32),
-        [VMEM, VMEM],
-    )(target, record_cell.reshape(1, records))
-    cells = lax.all_to_all(cells, "tile", split_axis=0, concat_axis=0, tiled=True)
-
-    mark = (classes + 1).astype(jnp.float32)
-
-    def edge(lo, hi, hlo, hhi):
-        return jnp.concatenate(
-            [anomaly[0, lo:hi], anomaly[1, lo:hi], mark[lo:hi], heights[hlo:hhi]], 0
-        )
-
-    before, after = exchange(
-        "tile",
-        edge(row_count - w, row_count, row_count - MAXSTEP, row_count),
-        edge(0, w, 0, MAXSTEP),
+
+    def room(*shape):
+        return pltpu.VMEM(shape, jnp.float32)
+
+    def sems(count):
+        return pltpu.SemaphoreType.DMA((2, count))
+
+    heights_all, base, cells = call(
+        functools.partial(heat_kernel, tiles, suns),
+        (
+            f32(suns, window + MAXSTEP, col_count),
+            f32(suns, row_count, col_count),
+            jax.ShapeDtypeStruct((tiles, 1, capacity), jnp.int32),
+        ),
+        [SMEM, SMEM] + [VMEM] * 6,
+        [
+            room(3, row_count, col_count),
+            room(2, 3, 8, col_count),
+            room(2, 3, 8, row_count),
+            room(2, 3, 8, row_count),
+            room(2, 2, 3, 8, LANE),
+            room(1, LANE),
+            room(suns, 1, LANE),
+            room(suns, row_count, col_count),
+            pltpu.VMEM((tiles, 1, capacity), jnp.int32),
+            sems(8),
+            sems(suns - 1),
+            sems(tiles - 1),
+            sems(3 * suns - 1),
+            sems(suns - 1),
+        ],
+        0,
+    )(
+        rate_table,
+        sun_radiation,
+        heights,
+        anomaly,
+        classes,
+        view_coef,
+        target,
+        record_cell.reshape(1, records),
     )
-    rows = jnp.stack(
-        [jnp.concatenate([after[i * w : (i + 1) * w], before[i * w : (i + 1) * w]], 0) for i in range(3)]
-    )
-    heights_ext = jnp.concatenate([before[3 * w :], heights, after[3 * w :]], 0)
-    heights_all = lax.all_gather(heights_ext, "sun", axis=0)
-
-    fields = jnp.concatenate([anomaly, mark[None]], 0)
-
-    def column(lo, hi):
-        return jnp.concatenate([fields[:, :, lo:hi], rows[:, :, lo:hi]], 1)
-
-    left, right = exchange("sun", column(col_count - w, col_count), column(0, w))
-    side = jnp.concatenate(
-        [right, jnp.zeros((3, row_count + 2 * w, LANE - 2 * w), jnp.float32), left], 2
-    )
-    radiation_all = lax.all_gather(sun_radiation[0], "sun", axis=0)
-    base = call(
-        functools.partial(heat_kernel, suns),
-        f32(suns, row_count, col_count),
-        [SMEM, SMEM] + [VMEM] * 5,
-    )(rate_table, radiation_all, anomaly, classes, rows, side, view_coef)
-    base = lax.all_to_all(base, "sun", split_axis=0, concat_axis=0, tiled=True)
-
-    group = 256
-    window = row_count + MAXSTEP
     radiant_block, sampled = call(
         sun_kernel,
-        (f32(1, row_count, cols), f32(tiles * capacity // group, group)),
+        (f32(1, row_count, cols), f32(tiles, 1, capacity)),
         [SMEM, SMEM] + [VMEM] * 3,
         [
-            pltpu.VMEM((2, window + 16, cols + 2 * LANE), jnp.float32),
+            room(2, window + 16, cols + 2 * LANE),
             pltpu.VMEM((cols, 3 * row_count), jnp.bfloat16),
         ],
-    )(sun_geometry, sun_radiation, heights_all, base, cells.reshape(-1, group))
-    returned = lax.all_to_all(
-        sampled.reshape(tiles, capacity), "tile", split_axis=0, concat_axis=0, tiled=True
-    )
-    excess = call(functools.partial(excess_kernel, tiles), f32(1, records), [VMEM] * 3)(
-        target, returned, record_air.reshape(1, records)
-    )
+    )(sun_geometry, sun_radiation, heights_all, base, cells)
+    excess = call(
+        functools.partial(excess_kernel, tiles, suns),
+        f32(1, records),
+        [VMEM] * 3,
+        [room(tiles, 1, capacity), sems(tiles - 1)],
+        1,
+    )(target, sampled, record_air.reshape(1, records))
     return radiant_block, excess.reshape(records)
 
 

time: 79.5 us -> 47.8 us (0.60)
  blocking collectives: 33.9 us -> 0 us
  Pallas kernels: 15.3 us -> 40.2 us
  starting transfers between devices: 21.6 us -> 0 us
  local copies, waits for them, and re-layouts: 5.21 us -> 6.56 us
  other arithmetic: 1.05 us -> 0 us
  waiting for transfers between devices: 0.89 us -> 0 us
    pallas_call x4 -> x3, Pallas kernels: 15.3 us -> 40.2 us  [the longest x1 24.4 us: on_device(): call(functools.partial(heat_kernel, tiles, suns), (f32(suns, window + MAX...]
    all_gather x2 -> x0, blocking collectives: 21.8 us -> none  [the longest x1 17.2 us: on_device(): heights_all = lax.all_gather(heights_ext, 'sun', axis=0)]
    all_to_all x1 -> x0, blocking collectives: 12.1 us -> none  [on_device(): lax.all_to_all(sampled.reshape(tiles, capacity), 'tile', split_axis=0, co...]
    all_to_all x2 -> x0, starting transfers between devices: 11.3 us -> none  [the longest x1 7.39 us: on_device(): lax.all_to_all(cells, 'tile', split_axis=0, concat_axis=0, tiled=True)]
    ppermute x4 -> x0, starting transfers between devices: 10.3 us -> none  [exchange(): return (lax.ppermute(last, axis, up), lax.ppermute(initial, axis, down))]
    unnamed x22 -> x21, local copies, waits for them, and re-layouts: 2.9 us -> 6.56 us
    slice x7 -> x0, local copies, waits for them, and re-layouts: 0.94 us -> none  [the longest x1 0.83 us: edge(): heights[hlo:hhi]]
    ppermute x4 -> x0, waiting for transfers between devices: 0.88 us -> none  [exchange(): return (lax.ppermute(last, axis, up), lax.ppermute(initial, axis, down))]
  transfers between devices with their start and end apart: 6 -> 0, of which waited for: 1 -> 0; matrix products, arithmetic and copies ran while one was open for 4% -> 0% of each run, Pallas kernels for 0% -> 0%
where the time goes in v2:
time: 47.8 us; the launch traced here: 47.4 us
  Pallas kernels  40.2 us (84%)
  local copies, waits for them, and re-layouts  6.56 us (14%)
  between operations  0.7 us (1%)
    pallas_call x1, Pallas kernels, on_device(): call(functools.partial(heat_kernel, tiles, suns), (f32(suns, window + MAX...  24.4 us
    pallas_call x1, Pallas kernels, on_device(): call(sun_kernel, (f32(1, row_count, cols), f32(tiles, 1, capacity)), [SME...  8.81 us
    pallas_call x1, Pallas kernels, on_device(): call(functools.partial(excess_kernel, tiles, suns), f32(1, records), [VME...  6.96 us
    unnamed x21, local copies, waits for them, and re-layouts  6.56 us

profile of v2, /device:TPU:0, one launch (start us, length us, event | category | flops | bytes accessed | tf_op | source)
XLA Modules:
  0.0 47.4 jit_solution(11207504958266315955)
XLA Ops:
  0.6 0.0 copy-start.4
  0.6 0.0 copy-start.7
  0.7 0.0 copy-start.8
  0.7 0.7 %copy-done.4 = s32[1024,1]{0,1:T(1,128)S(1)} copy-done((s32[1024,1]{0,1:T(1,128)S(1)}, s32[1024,1]{0,1:T(1,128)}, u32[]{:S(2)}) %copy-start.4) | copy-done | bytes 4120
  1.3 0.0 copy-done.7
  1.3 0.0 copy-done.8
  1.3 0.0 copy-start
  1.3 1.0 %copy-done = f32[2,128,512]{2,1,0:T(8,128)S(1)} copy-done((f32[2,128,512]{2,1,0:T(8,128)S(1)}, f32[2,128,512]{2,1,0:T(8,128)}, u32[]{:S(2)}) %copy-start) | copy-done | bytes 524312
  2.4 0.0 copy-start.1
  2.4 1.0 %copy-done.1 = bf16[3,128,512]{2,1,0:T(8,128)(2,1)S(1)} copy-done((bf16[3,128,512]{2,1,0:T(8,128)(2,1)S(1)}, bf16[3,128,512]{2,1,0:T(8,128)(2,1)}, u32[]{:S(2)}) %copy-start.1) | copy-done | bytes 393240
  3.4 0.0 copy-start.2
  3.4 0.9 %copy-done.2 = f32[128,512]{1,0:T(8,128)S(1)} copy-done((f32[128,512]{1,0:T(8,128)S(1)}, f32[128,512]{1,0:T(8,128)}, u32[]{:S(2)}) %copy-start.2) | copy-done | bytes 262168
  4.3 0.0 copy-start.3
  4.3 0.9 %copy-done.3 = s32[128,512]{1,0:T(8,128)S(1)} copy-done((s32[128,512]{1,0:T(8,128)S(1)}, s32[128,512]{1,0:T(8,128)}, u32[]{:S(2)}) %copy-start.3) | copy-done | bytes 262168
  5.3 0.0 copy-start.5
  5.3 0.7 %copy-done.5 = s32[1024]{0:T(1024)S(1)} copy-done((s32[1024]{0:T(1024)S(1)}, s32[1024]{0:T(1024)}, u32[]{:S(2)}) %copy-start.5) | copy-done | bytes 4120
  6.0 24.4 %shard_map.113 = (f32[2,176,512]{2,1,0:T(8,128)S(1)}, f32[2,128,512]{2,1,0:T(8,128)S(1)}, s32[16,1,128]{2,1,0:T(1,128)S(1)}) custom-call(f32[2,16]{1,0:T(2,128)S(1)} %copy-done.8, f32[1,3]{1,0:T(1,128)S(1)} %copy-done.7, f32[128,512]{1,0:T(8,128)S(1)} %copy-done.2, f32[2,128,512]{2,1,0:T(8,128)S(1)} %copy-done, s32[128,512]{1,0:T(8,128)S(1)} %copy-done.3, ...), custom_call_target="tpu_custom_call" | custom-call | tf_op jit(solution)/shard_map/pallas_call | solution.py:415
  30.4 0.0 copy-start.9
  30.4 0.6 %copy-done.9 = s32[1,4]{1,0:T(1,128)S(1)} copy-done((s32[1,4]{1,0:T(1,128)S(1)}, s32[1,4]{1,0:T(1,128)}, u32[]{:S(2)}) %copy-start.9) | copy-done | bytes 40
  31.1 0.0 copy-start.6
  31.1 8.8 %shard_map.114 = (f32[1,128,1024]{2,1,0:T(8,128)}, f32[16,1,128]{2,1,0:T(1,128)S(1)}) custom-call(s32[1,4]{1,0:T(1,128)S(1)} %copy-done.9, f32[1,3]{1,0:T(1,128)S(1)} %copy-done.7, f32[2,176,512]{2,1,0:T(8,128)S(1)} %get-tuple-element.7.heights_ref, f32[2,128,512]{2,1,0:T(8,128)S(1)} %get-tuple-element.8.base_ref, s32[16,1,128]{2,1,0:T(1,128)S(1)} %get-tuple-element.9.cells_ref), custom_call_target="tpu_custom_call" | custom-call | tf_op jit(solution)/shard_map/pallas_call | solution.py:450
  39.9 0.0 copy-done.6
  39.9 7.0 %shard_map.115 = f32[1,1024]{1,0:T(1,128)S(1)} custom-call(s32[1,1024]{1,0:T(1,128)S(1)} %bitcast.5, f32[16,1,128]{2,1,0:T(1,128)S(1)} %get-tuple-element.11.sampled_ref, f32[1,1024]{1,0:T(1,128)S(1)} %bitcast.8), custom_call_target="tpu_custom_call" | custom-call | tf_op jit(solution)/shard_map/pallas_call | solution.py:459
  46.9 0.6 %copy.13 = f32[1024]{0:T(1024)} copy(f32[1024]{0:T(1024)S(1)} %bitcast.6) | data formatting | bytes 8192
Async XLA Ops:
  0.6 0.7 %copy-start.4 = (s32[1024,1]{0,1:T(1,128)S(1)}, s32[1024,1]{0,1:T(1,128)}, u32[]{:S(2)}) copy-start(s32[1024,1]{0,1:T(1,128)} %param.17) | copy-start | bytes 12292
  0.6 0.7 %copy-start.7 = (f32[1,3]{1,0:T(1,128)S(1)}, f32[1,3]{1,0:T(1,128)}, u32[]{:S(2)}) copy-start(f32[1,3]{1,0:T(1,128)} %sun_ref.3) | copy-start | bytes 40
  0.7 0.7 %copy-start.8 = (f32[2,16]{1,0:T(2,128)S(1)}, f32[2,16]{1,0:T(2,128)}, u32[]{:S(2)}) copy-start(f32[2,16]{1,0:T(2,128)} %table_ref.1) | copy-start | bytes 388
  1.3 1.0 %copy-start = (f32[2,128,512]{2,1,0:T(8,128)S(1)}, f32[2,128,512]{2,1,0:T(8,128)}, u32[]{:S(2)}) copy-start(f32[2,128,512]{2,1,0:T(8,128)} %anomaly_ref.1) | copy-start | bytes 1572868
  2.4 1.0 %copy-start.1 = (bf16[3,128,512]{2,1,0:T(8,128)(2,1)S(1)}, bf16[3,128,512]{2,1,0:T(8,128)(2,1)}, u32[]{:S(2)}) copy-start(bf16[3,128,512]{2,1,0:T(8,128)(2,1)} %view_ref.1) | copy-start | bytes 1179652
  3.4 0.9 %copy-start.2 = (f32[128,512]{1,0:T(8,128)S(1)}, f32[128,512]{1,0:T(8,128)}, u32[]{:S(2)}) copy-start(f32[128,512]{1,0:T(8,128)} %heights_ref.1) | copy-start | bytes 786436
  4.3 0.9 %copy-start.3 = (s32[128,512]{1,0:T(8,128)S(1)}, s32[128,512]{1,0:T(8,128)}, u32[]{:S(2)}) copy-start(s32[128,512]{1,0:T(8,128)} %class_ref.1) | copy-start | bytes 786436
  5.3 0.7 %copy-start.5 = (s32[1024]{0:T(1024)S(1)}, s32[1024]{0:T(1024)}, u32[]{:S(2)}) copy-start(s32[1024]{0:T(1024)} %param.18) | copy-start | bytes 12292
  30.4 0.7 %copy-start.9 = (s32[1,4]{1,0:T(1,128)S(1)}, s32[1,4]{1,0:T(1,128)}, u32[]{:S(2)}) copy-start(s32[1,4]{1,0:T(1,128)} %geometry_ref.1) | copy-start | bytes 52
  31.1 8.8 %copy-start.6 = (f32[1024]{0:T(1024)S(1)}, f32[1024]{0:T(1024)}, u32[]{:S(2)}) copy-start(f32[1024]{0:T(1024)} %param.19) | copy-start | bytes 12292

commit v3 on v2

--- a/solution.py
+++ b/solution.py
@@ -75,14 +75,15 @@
         pl.semaphore_signal(
             barrier, inc=1, device_id=peer, device_id_type=pl.DeviceIdType.MESH
         )
-    pl.semaphore_wait(barrier, len(peers))
+    return lambda: pl.semaphore_wait(barrier, len(peers))
 
 
 def heat_kernel(
-    tiles, suns, table_ref, sun_ref, heights_ref, anomaly_ref, class_ref, view_ref, tile_ref, cell_ref,
+    tiles, suns, table_ref, sun_ref, heights_ref, anomaly_hbm, class_hbm, view_hbm, tile_hbm, cell_hbm,
     heights_all, base_all, cells_in,
     fields, rows_in, cols_out, cols_in, corners_in, light_out, light_in, base_out, cells_out,
-    near_sems, light_sems, cell_sems, height_sems, base_sems,
+    class_ref, view_ref, tile_ref, cell_ref,
+    near_sems, light_sems, cell_sems, height_sems, base_sems, load_sems,
 ):
     row_count, col_count = class_ref.shape
     capacity = cells_in.shape[2]
@@ -92,8 +93,27 @@
     other_tiles = [lax.rem(tile + k, tiles) for k in range(1, tiles)]
     other_suns = [lax.rem(sun + k, suns) for k in range(1, suns)]
 
-    fields[0] = anomaly_ref[0]
-    fields[1] = anomaly_ref[1]
+    wait_peers = greet(
+        [(t, sun) for t in other_tiles]
+        + [(t, s) for s in other_suns for t in (above, tile, below)]
+    )
+    loads = [
+        pltpu.make_async_copy(src, dst, load_sems.at[k])
+        for k, (src, dst) in enumerate(
+            [
+                (class_hbm, class_ref),
+                (anomaly_hbm, fields.at[pl.ds(0, 2)]),
+                (tile_hbm, tile_ref),
+                (cell_hbm, cell_ref),
+                (view_hbm, view_ref),
+                (heights_ref, heights_all.at[sun, pl.ds(MAXSTEP, row_count), :]),
+            ]
+        )
+    ]
+    for load in loads:
+        load.start()
+    loads[0].wait()
+    loads[1].wait()
     fields[2] = (class_ref[...] + 1).astype(jnp.float32)
     last = col_count - LANE
     for i in range(3):
@@ -106,10 +126,7 @@
     light_out[...] = light
     light_in[sun] = light
 
-    greet(
-        [(t, sun) for t in other_tiles]
-        + [(t, s) for s in other_suns for t in (above, tile, below)]
-    )
+    wait_peers()
     top, bottom = pl.ds(0, 8), pl.ds(row_count - 8, 8)
     first_cols, last_cols = pl.ds(0, LANE), pl.ds(last, LANE)
     near = [
@@ -150,8 +167,8 @@
         )
     for copy in far:
         copy.start()
-    heights_all[sun, MAXSTEP : MAXSTEP + row_count, :] = heights_ref[...]
-
+    for load in loads[2:]:
+        load.wait()
     cells = bucket(tiles, capacity, tile_ref, cell_ref)
     for t in range(tiles):
         cells_out[t] = cells[t : t + 1]
@@ -348,7 +365,7 @@
 def excess_kernel(tiles, suns, tile_ref, sampled_ref, air_ref, excess_ref, returned, sems):
     tile, sun = lax.axis_index("tile"), lax.axis_index("sun")
     others = [lax.rem(tile + k, tiles) for k in range(1, tiles)]
-    greet([(t, sun) for t in others])
+    greet([(t, sun) for t in others])()
     copies = [
         remote(sampled_ref.at[t], returned.at[tile], sems, k, t, sun) for k, t in enumerate(others)
     ]
@@ -419,7 +436,7 @@
             f32(suns, row_count, col_count),
             jax.ShapeDtypeStruct((tiles, 1, capacity), jnp.int32),
         ),
-        [SMEM, SMEM] + [VMEM] * 6,
+        [SMEM, SMEM] + [pl.BlockSpec(memory_space=pl.ANY)] * 6,
         [
             room(3, row_count, col_count),
             room(2, 3, 8, col_count),
@@ -430,11 +447,16 @@
             room(suns, 1, LANE),
             room(suns, row_count, col_count),
             pltpu.VMEM((tiles, 1, capacity), jnp.int32),
+            pltpu.VMEM(classes.shape, jnp.int32),
+            pltpu.VMEM(view_coef.shape, view_coef.dtype),
+            pltpu.VMEM((1, records), jnp.int32),
+            pltpu.VMEM((1, records), jnp.int32),
             sems(8),
             sems(suns - 1),
             sems(tiles - 1),
             sems(3 * suns - 1),
             sems(suns - 1),
+            pltpu.SemaphoreType.DMA((6,)),
         ],
         0,
     )(

time: 47.8 us -> 47.7 us (level)
  no operation moved by 1% of the time
where the time goes in v3:
time: 47.7 us; the launch traced here: 47.4 us
  Pallas kernels  40.1 us (84%)
  local copies, waits for them, and re-layouts  6.56 us (14%)
  between operations  0.7 us (1%)
    pallas_call x1, Pallas kernels, on_device(): call(functools.partial(heat_kernel, tiles, suns), (f32(suns, window + MAX...  24.4 us
    pallas_call x1, Pallas kernels, on_device(): call(sun_kernel, (f32(1, row_count, cols), f32(tiles, 1, capacity)), [SME...  8.81 us
    pallas_call x1, Pallas kernels, on_device(): call(functools.partial(excess_kernel, tiles, suns), f32(1, records), [VME...  6.96 us
    unnamed x21, local copies, waits for them, and re-layouts  6.56 us

profile of v3, /device:TPU:0, one launch (start us, length us, event | category | flops | bytes accessed | tf_op | source)
XLA Modules:
  0.0 47.4 jit_solution(10200430711524503598)
XLA Ops:
  0.6 0.0 copy-start.4
  0.6 0.0 copy-start.7
  0.7 0.0 copy-start.8
  0.7 0.7 %copy-done.4 = s32[1024,1]{0,1:T(1,128)S(1)} copy-done((s32[1024,1]{0,1:T(1,128)S(1)}, s32[1024,1]{0,1:T(1,128)}, u32[]{:S(2)}) %copy-start.4) | copy-done | bytes 4120
  1.3 0.0 copy-done.7
  1.3 0.0 copy-done.8
  1.3 0.0 copy-start
  1.3 1.0 %copy-done = f32[2,128,512]{2,1,0:T(8,128)S(1)} copy-done((f32[2,128,512]{2,1,0:T(8,128)S(1)}, f32[2,128,512]{2,1,0:T(8,128)}, u32[]{:S(2)}) %copy-start) | copy-done | bytes 524312
  2.4 0.0 copy-start.1
  2.4 1.0 %copy-done.1 = bf16[3,128,512]{2,1,0:T(8,128)(2,1)S(1)} copy-done((bf16[3,128,512]{2,1,0:T(8,128)(2,1)S(1)}, bf16[3,128,512]{2,1,0:T(8,128)(2,1)}, u32[]{:S(2)}) %copy-start.1) | copy-done | bytes 393240
  3.4 0.0 copy-start.2
  3.4 0.9 %copy-done.2 = f32[128,512]{1,0:T(8,128)S(1)} copy-done((f32[128,512]{1,0:T(8,128)S(1)}, f32[128,512]{1,0:T(8,128)}, u32[]{:S(2)}) %copy-start.2) | copy-done | bytes 262168
  4.3 0.0 copy-start.3
  4.3 0.9 %copy-done.3 = s32[128,512]{1,0:T(8,128)S(1)} copy-done((s32[128,512]{1,0:T(8,128)S(1)}, s32[128,512]{1,0:T(8,128)}, u32[]{:S(2)}) %copy-start.3) | copy-done | bytes 262168
  5.3 0.0 copy-start.5
  5.3 0.7 %copy-done.5 = s32[1024]{0:T(1024)S(1)} copy-done((s32[1024]{0:T(1024)S(1)}, s32[1024]{0:T(1024)}, u32[]{:S(2)}) %copy-start.5) | copy-done | bytes 4120
  6.0 24.4 %shard_map.113 = (f32[2,176,512]{2,1,0:T(8,128)S(1)}, f32[2,128,512]{2,1,0:T(8,128)S(1)}, s32[16,1,128]{2,1,0:T(1,128)S(1)}) custom-call(f32[2,16]{1,0:T(2,128)S(1)} %copy-done.8, f32[1,3]{1,0:T(1,128)S(1)} %copy-done.7, f32[128,512]{1,0:T(8,128)S(1)} %copy-done.2, f32[2,128,512]{2,1,0:T(8,128)S(1)} %copy-done, s32[128,512]{1,0:T(8,128)S(1)} %copy-done.3, ...), custom_call_target="tpu_custom_call" | custom-call | tf_op jit(solution)/shard_map/pallas_call | solution.py:432
  30.3 0.0 copy-start.9
  30.3 0.6 %copy-done.9 = s32[1,4]{1,0:T(1,128)S(1)} copy-done((s32[1,4]{1,0:T(1,128)S(1)}, s32[1,4]{1,0:T(1,128)}, u32[]{:S(2)}) %copy-start.9) | copy-done | bytes 40
  31.0 0.0 copy-start.6
  31.0 8.8 %shard_map.114 = (f32[1,128,1024]{2,1,0:T(8,128)}, f32[16,1,128]{2,1,0:T(1,128)S(1)}) custom-call(s32[1,4]{1,0:T(1,128)S(1)} %copy-done.9, f32[1,3]{1,0:T(1,128)S(1)} %copy-done.7, f32[2,176,512]{2,1,0:T(8,128)S(1)} %get-tuple-element.7.heights_ref, f32[2,128,512]{2,1,0:T(8,128)S(1)} %get-tuple-element.8.base_ref, s32[16,1,128]{2,1,0:T(1,128)S(1)} %get-tuple-element.9.cells_ref), custom_call_target="tpu_custom_call" | custom-call | tf_op jit(solution)/shard_map/pallas_call | solution.py:472
  39.8 0.0 copy-done.6
  39.8 7.0 %shard_map.115 = f32[1,1024]{1,0:T(1,128)S(1)} custom-call(s32[1,1024]{1,0:T(1,128)S(1)} %bitcast.5, f32[16,1,128]{2,1,0:T(1,128)S(1)} %get-tuple-element.11.sampled_ref, f32[1,1024]{1,0:T(1,128)S(1)} %bitcast.8), custom_call_target="tpu_custom_call" | custom-call | tf_op jit(solution)/shard_map/pallas_call | solution.py:481
  46.8 0.6 %copy.13 = f32[1024]{0:T(1024)} copy(f32[1024]{0:T(1024)S(1)} %bitcast.6) | data formatting | bytes 8192
Async XLA Ops:
  0.6 0.7 %copy-start.4 = (s32[1024,1]{0,1:T(1,128)S(1)}, s32[1024,1]{0,1:T(1,128)}, u32[]{:S(2)}) copy-start(s32[1024,1]{0,1:T(1,128)} %param.17) | copy-start | bytes 12292
  0.6 0.7 %copy-start.7 = (f32[1,3]{1,0:T(1,128)S(1)}, f32[1,3]{1,0:T(1,128)}, u32[]{:S(2)}) copy-start(f32[1,3]{1,0:T(1,128)} %sun_ref.3) | copy-start | bytes 40
  0.7 0.7 %copy-start.8 = (f32[2,16]{1,0:T(2,128)S(1)}, f32[2,16]{1,0:T(2,128)}, u32[]{:S(2)}) copy-start(f32[2,16]{1,0:T(2,128)} %table_ref.1) | copy-start | bytes 388
  1.3 1.0 %copy-start = (f32[2,128,512]{2,1,0:T(8,128)S(1)}, f32[2,128,512]{2,1,0:T(8,128)}, u32[]{:S(2)}) copy-start(f32[2,128,512]{2,1,0:T(8,128)} %anomaly_hbm.1) | copy-start | bytes 1572868
  2.4 1.0 %copy-start.1 = (bf16[3,128,512]{2,1,0:T(8,128)(2,1)S(1)}, bf16[3,128,512]{2,1,0:T(8,128)(2,1)}, u32[]{:S(2)}) copy-start(bf16[3,128,512]{2,1,0:T(8,128)(2,1)} %view_hbm.1) | copy-start | bytes 1179652
  3.4 0.9 %copy-start.2 = (f32[128,512]{1,0:T(8,128)S(1)}, f32[128,512]{1,0:T(8,128)}, u32[]{:S(2)}) copy-start(f32[128,512]{1,0:T(8,128)} %heights_ref.1) | copy-start | bytes 786436
  4.3 0.9 %copy-start.3 = (s32[128,512]{1,0:T(8,128)S(1)}, s32[128,512]{1,0:T(8,128)}, u32[]{:S(2)}) copy-start(s32[128,512]{1,0:T(8,128)} %class_hbm.1) | copy-start | bytes 786436
  5.3 0.7 %copy-start.5 = (s32[1024]{0:T(1024)S(1)}, s32[1024]{0:T(1024)}, u32[]{:S(2)}) copy-start(s32[1024]{0:T(1024)} %param.18) | copy-start | bytes 12292
  30.3 0.7 %copy-start.9 = (s32[1,4]{1,0:T(1,128)S(1)}, s32[1,4]{1,0:T(1,128)}, u32[]{:S(2)}) copy-start(s32[1,4]{1,0:T(1,128)} %geometry_ref.1) | copy-start | bytes 52
  31.0 8.8 %copy-start.6 = (f32[1024]{0:T(1024)S(1)}, f32[1024]{0:T(1024)}, u32[]{:S(2)}) copy-start(f32[1024]{0:T(1024)} %param.19) | copy-start | bytes 12292

commit v4 on v3

--- a/solution.py
+++ b/solution.py
@@ -13,7 +13,7 @@
 BASE_KELVIN = 300.0
 ZERO_CELSIUS = 273.15
 LANE = 128
-VMEM_LIMIT = 50 * 2**20
+VMEM_LIMIT = 64 * 2**20
 
 VMEM = pl.BlockSpec(memory_space=pltpu.VMEM)
 SMEM = pl.BlockSpec(memory_space=pltpu.SMEM)
@@ -436,7 +436,7 @@
             f32(suns, row_count, col_count),
             jax.ShapeDtypeStruct((tiles, 1, capacity), jnp.int32),
         ),
-        [SMEM, SMEM] + [pl.BlockSpec(memory_space=pl.ANY)] * 6,
+        [SMEM, SMEM] + [pl.BlockSpec(memory_space=pltpu.HBM)] * 6,
         [
             room(3, row_count, col_count),
             room(2, 3, 8, col_count),

time: 47.7 us -> 46 us (0.964)
  local copies, waits for them, and re-layouts: 6.56 us -> 1.26 us
  Pallas kernels: 40.1 us -> 43.8 us
    unnamed x21 -> x1, local copies, waits for them, and re-layouts: 6.56 us -> 1.26 us
    pallas_call x1, Pallas kernels: 8.81 us -> 10.2 us  [on_device(): call(sun_kernel, (f32(1, row_count, cols), f32(tiles, 1, capacity)), [SME...]
    pallas_call x1, Pallas kernels: 24.4 us -> 25.6 us  [on_device(): call(functools.partial(heat_kernel, tiles, suns), (f32(suns, window + MAX...]
    pallas_call x1, Pallas kernels: 6.96 us -> 8.1 us  [on_device(): call(functools.partial(excess_kernel, tiles, suns), f32(1, records), [VME...]
where the time goes in v4:
time: 46 us; the launch traced here: 45.7 us
  Pallas kernels  43.8 us (95%)
  local copies, waits for them, and re-layouts  1.26 us (3%)
  between operations  0.65 us (1%)
    pallas_call x1, Pallas kernels, on_device(): call(functools.partial(heat_kernel, tiles, suns), (f32(suns, window + MAX...  25.6 us
    pallas_call x1, Pallas kernels, on_device(): call(sun_kernel, (f32(1, row_count, cols), f32(tiles, 1, capacity)), [SME...  10.2 us
    pallas_call x1, Pallas kernels, on_device(): call(functools.partial(excess_kernel, tiles, suns), f32(1, records), [VME...  8.1 us
    unnamed x1, local copies, waits for them, and re-layouts  1.26 us

profile of v4, /device:TPU:0, one launch (start us, length us, event | category | flops | bytes accessed | tf_op | source)
XLA Modules:
  0.0 45.7 jit_solution(394732458427899677)
XLA Ops:
  0.6 25.6 %shard_map.113 = (f32[2,176,512]{2,1,0:T(8,128)}, f32[2,128,512]{2,1,0:T(8,128)}, s32[16,1,128]{2,1,0:T(1,128)}) custom-call(f32[2,16]{1,0:T(2,128)} %table_ref.1, f32[1,3]{1,0:T(1,128)} %sun_ref.3, f32[128,512]{1,0:T(8,128)} %heights_ref.1, f32[2,128,512]{2,1,0:T(8,128)} %anomaly_hbm.1, s32[128,512]{1,0:T(8,128)} %class_hbm.1, ...), custom_call_target="tpu_custom_call" | custom-call | tf_op jit(solution)/shard_map/pallas_call | solution.py:432
  26.2 10.2 %shard_map.114 = (f32[1,128,1024]{2,1,0:T(8,128)}, f32[16,1,128]{2,1,0:T(1,128)}) custom-call(s32[1,4]{1,0:T(1,128)} %geometry_ref.1, f32[1,3]{1,0:T(1,128)} %sun_ref.3, f32[2,176,512]{2,1,0:T(8,128)} %get-tuple-element.7.heights_ref, f32[2,128,512]{2,1,0:T(8,128)} %get-tuple-element.8.base_ref, s32[16,1,128]{2,1,0:T(1,128)} %get-tuple-element.9.cells_ref), custom_call_target="tpu_custom_call" | custom-call | tf_op jit(solution)/shard_map/pallas_call | solution.py:472
  36.4 8.1 %shard_map.115 = f32[1,1024]{1,0:T(1,128)} custom-call(s32[1,1024]{1,0:T(1,128)} %bitcast.5, f32[16,1,128]{2,1,0:T(1,128)} %get-tuple-element.11.sampled_ref, f32[1,1024]{1,0:T(1,128)} %bitcast.8), custom_call_target="tpu_custom_call" | custom-call | tf_op jit(solution)/shard_map/pallas_call | solution.py:481
  44.5 1.3 %copy.13 = f32[1024]{0:T(1024)} copy(f32[1024]{0:T(1024)} %bitcast.6) | data formatting | bytes 8192
